TPU v7x, 256 devices: a whole 4x4x8 slice. The times are simulated.
256 devices in a mesh: dp: 2 (over x_lo), outer: 8 (over z), inner: 16 (over x_hi, y, core).
Axes of the slice: x: 4 (x_hi: 2, x_lo: 2; x = x_hi * 2 + x_lo), y: 4, z: 8, core: 2. Of those that a mesh axis runs over, the one named last changes fastest.
Arguments:
- queries: bfloat16 [65536, 1024], P(('dp', 'outer', 'inner')), parts along dimension 0, may hold values from -6 to 6
- keys: bfloat16 [65536, 128], P(('dp', 'outer', 'inner')), parts along dimension 0, may hold values from -6 to 6
- values: bfloat16 [65536, 128], P(('dp', 'outer', 'inner')), parts along dimension 0, may hold values from -6 to 6
- outputs: bfloat16 [65536, 1024], P(('dp', 'outer', 'inner')), parts along dimension 0, may hold values from -6 to 6
- out_grads: bfloat16 [65536, 1024], P(('dp', 'outer', 'inner')), parts along dimension 0, may hold values from -6 to 6
- log_sums: float32 [8, 65536], P(None, ('dp', 'outer', 'inner')), parts along dimension 1, may hold values from 6 to 9
- doc_lengths: int32 [64], P('dp'), parts along dimension 0, may hold values from 1 to 2048, 32768 in all
Outputs:
- query_grads: bfloat16 [65536, 1024], P(('dp', 'outer', 'inner')), parts along dimension 0
- key_grads: bfloat16 [65536, 128], P(('dp', 'outer', 'inner')), parts along dimension 0
- value_grads: bfloat16 [65536, 128], P(('dp', 'outer', 'inner')), parts along dimension 0
There are 2 independent parts, one for each index of `dp`. A program takes and returns all parts, laid end to end along the dimension named above; each array names one. Nothing has to cross between parts.
Inputs may be any that keep to these rules, and one draw needn't show every extreme that they name: `doc_lengths`: each length is at least 1 and at most 2048, the lengths sum to 32768, and some document has exactly 2048 tokens.
All inputs are finite; a program needn't handle non-finite values.
Results may differ from a plain program's by a relative error of at most 0.01.
Values may be sent and summed in bfloat16 or wider, within the bound.
A program may use at most 64 MiB of HBM per device.

v0:
```python
import jax
import jax.numpy as jnp
from jax import lax
from jax.sharding import PartitionSpec as P

SPAN = 8


def passed_along(value, axis, steps):
    count = lax.axis_size(axis)
    initial, last = (max(0, -steps), min(count, count - steps))
    return lax.ppermute(value, axis, [(source, source + steps) for source in range(initial, last)])


def doc_index(ends, positions):
    return jnp.sum((ends[None, :] <= positions[:, None]).astype(jnp.int32), axis=1)


def local(queries, keys, values, outputs, out_grads, log_sums, doc_lengths):
    tok_rows = keys.shape[0]
    width = keys.shape[1]
    heads = log_sums.shape[0]
    scale = 1.0 / width**0.5
    here = lax.axis_index(("outer", "inner"))
    ends = jnp.cumsum(doc_lengths)
    rows = jnp.arange(tok_rows, dtype=jnp.int32)
    qpos = here * tok_rows + rows
    qdoc = doc_index(ends, qpos)
    q_heads = queries.reshape(tok_rows, heads, width)
    g_heads = out_grads.reshape(tok_rows, heads, width)
    delta = jnp.sum(
        g_heads.astype(jnp.float32) * outputs.reshape(tok_rows, heads, width).astype(jnp.float32),
        axis=2,
    )

    def pair_terms(stacked, back):
        kblock = stacked[0]
        vblock = stacked[1]
        kpos = (here - back) * tok_rows + rows
        kdoc = doc_index(ends, kpos)
        allowed = (
            (kpos[None, :] <= qpos[:, None])
            & (kdoc[None, :] == qdoc[:, None])
            & (kpos[None, :] >= 0)
        )
        scores = (
            jnp.einsum("qhd,kd->hqk", q_heads, kblock, preferred_element_type=jnp.float32) * scale
        )
        prob = jnp.where(allowed[None], jnp.exp(scores - log_sums[:, :, None]), 0.0)
        prob_low = prob.astype(jnp.bfloat16)
        dv = jnp.einsum("hqk,qhd->kd", prob_low, g_heads, preferred_element_type=jnp.float32)
        dprob = jnp.einsum("qhd,kd->hqk", g_heads, vblock, preferred_element_type=jnp.float32)
        dscore = (prob * (dprob - delta.T[:, :, None])).astype(jnp.bfloat16)
        dq = jnp.einsum("hqk,kd->qhd", dscore, kblock, preferred_element_type=jnp.float32) * scale
        dk = jnp.einsum("hqk,qhd->kd", dscore, q_heads, preferred_element_type=jnp.float32) * scale
        return (dq, jnp.stack([dk, dv]))

    kv_pair = jnp.stack([keys, values])
    dq_total, own_grads = pair_terms(kv_pair, 0)
    for back in range(1, SPAN + 1):
        arrived = passed_along(kv_pair, ("outer", "inner"), back)
        dq_part, grad_part = pair_terms(arrived, back)
        dq_total = dq_total + dq_part
        own_grads = own_grads + passed_along(
            grad_part.astype(jnp.bfloat16), ("outer", "inner"), -back
        ).astype(grad_part.dtype)
    query_grads = dq_total.reshape(tok_rows, heads * width).astype(jnp.bfloat16)
    return (query_grads, own_grads[0].astype(jnp.bfloat16), own_grads[1].astype(jnp.bfloat16))


def solution(mesh):
    placed = (
        P(("dp", "outer", "inner"), None),
        P(("dp", "outer", "inner"), None),
        P(("dp", "outer", "inner"), None),
        P(("dp", "outer", "inner"), None),
        P(("dp", "outer", "inner"), None),
        P(None, ("dp", "outer", "inner")),
        P("dp"),
    )
    return jax.shard_map(
        local,
        mesh=mesh,
        in_specs=placed,
        out_specs=(
            P(("dp", "outer", "inner"), None),
            P(("dp", "outer", "inner"), None),
            P(("dp", "outer", "inner"), None),
        ),
        check_vma=False,
    )
```

profile of v0, /device:TPU:182, one launch (start us, length us, event | category | flops | bytes accessed | tf_op | source)
XLA Modules:
  0.0 114.8 jit_solution(7494437046100157671)
XLA Ops:
  0.6 0.9 pad_maximum_fusion
  1.6 3.8 %collective-permute-start.7 = (bf16[2,256,128]{2,1,0:T(8,128)(2,1)S(1)}, bf16[2,256,128]{2,1,0:T(8,128)(2,1)S(1)}, u32[]{:S(2)}, u32[]{:S(2)}) collective-permute-start(bf16[2,256,128]{2,1,0:T(8,128)(2,1)S(1)} %pad_maximum_fusion), channel_id=1, source_target_pairs={{0,8},{1,9},{2,10},{3,11},{4,12},{5,13},{6,14},{7,15},{8,16},{9,17... | collective-permute-start | bytes 393224 | tf_op jit(solution)/shard_map/ppermute | solution.py:12
  5.4 3.1 %collective-permute-start.6 = (bf16[2,256,128]{2,1,0:T(8,128)(2,1)S(1)}, bf16[2,256,128]{2,1,0:T(8,128)(2,1)S(1)}, u32[]{:S(2)}, u32[]{:S(2)}) collective-permute-start(bf16[2,256,128]{2,1,0:T(8,128)(2,1)S(1)} %pad_maximum_fusion), channel_id=1, source_target_pairs={{0,7},{1,8},{2,9},{3,10},{4,11},{5,12},{6,13},{7,14},{8,15},{9,16}... | collective-permute-start | bytes 393224 | tf_op jit(solution)/shard_map/ppermute | solution.py:12
  8.5 3.7 %collective-permute-start.5 = (bf16[2,256,128]{2,1,0:T(8,128)(2,1)S(1)}, bf16[2,256,128]{2,1,0:T(8,128)(2,1)S(1)}, u32[]{:S(2)}, u32[]{:S(2)}) collective-permute-start(bf16[2,256,128]{2,1,0:T(8,128)(2,1)S(1)} %pad_maximum_fusion), channel_id=1, source_target_pairs={{0,6},{1,7},{2,8},{3,9},{4,10},{5,11},{6,12},{7,13},{8,14},{9,15},... | collective-permute-start | bytes 393224 | tf_op jit(solution)/shard_map/ppermute | solution.py:12
  12.1 5.2 %collective-permute-start.4 = (bf16[2,256,128]{2,1,0:T(8,128)(2,1)S(1)}, bf16[2,256,128]{2,1,0:T(8,128)(2,1)S(1)}, u32[]{:S(2)}, u32[]{:S(2)}) collective-permute-start(bf16[2,256,128]{2,1,0:T(8,128)(2,1)S(1)} %pad_maximum_fusion), channel_id=1, source_target_pairs={{0,5},{1,6},{2,7},{3,8},{4,9},{5,10},{6,11},{7,12},{8,13},{9,14},{... | collective-permute-start | bytes 393224 | tf_op jit(solution)/shard_map/ppermute | solution.py:12
  17.3 4.1 %collective-permute-start.3 = (bf16[2,256,128]{2,1,0:T(8,128)(2,1)S(1)}, bf16[2,256,128]{2,1,0:T(8,128)(2,1)S(1)}, u32[]{:S(2)}, u32[]{:S(2)}) collective-permute-start(bf16[2,256,128]{2,1,0:T(8,128)(2,1)S(1)} %pad_maximum_fusion), channel_id=1, source_target_pairs={{0,4},{1,5},{2,6},{3,7},{4,8},{5,9},{6,10},{7,11},{8,12},{9,13},{1... | collective-permute-start | bytes 393224 | tf_op jit(solution)/shard_map/ppermute | solution.py:12
  21.6 0.7 copy.179
  22.5 1.1 copy.265
  23.6 1.1 %convert_bitcast_fusion = f32[32,8,8,128]{3,1,2,0:T(8,128)S(1)} fusion(bf16[256,1024]{1,0:T(8,128)(2,1)} %param.10), kind=kLoop, calls=%fused_computation.141 | loop fusion | flops 262144 | bytes 1572864
  25.6 0.9 and_and_fusion
  26.5 0.6 fusion.35
  27.2 0.5 convolution_bitcast_fusion.16
  28.0 0.4 fusion.33
  28.8 0.5 and_and_fusion.1
  29.4 0.4 fusion.63
  29.8 1.9 %collective-permute-start = (bf16[2,256,128]{2,1,0:T(8,128)(2,1)S(1)}, bf16[2,256,128]{2,1,0:T(8,128)(2,1)S(1)}, u32[]{:S(2)}, u32[]{:S(2)}) collective-permute-start(bf16[2,256,128]{2,1,0:T(8,128)(2,1)S(1)} %pad_maximum_fusion), channel_id=1, source_target_pairs={{0,1},{1,2},{2,3},{3,4},{4,5},{5,6},{6,7},{7,8},{8,9},{9,10},{10,1... | collective-permute-start | bytes 393224 | tf_op jit(solution)/shard_map/ppermute | solution.py:12
  31.7 0.6 fusion.3
  32.4 0.5 fusion.80
  32.8 0.5 fusion.1
  33.3 0.4 fusion.88
  33.7 2.4 %collective-permute-done = bf16[2,256,128]{2,1,0:T(8,128)(2,1)S(1)} collective-permute-done((bf16[2,256,128]{2,1,0:T(8,128)(2,1)S(1)}, bf16[2,256,128]{2,1,0:T(8,128)(2,1)S(1)}, u32[]{:S(2)}, u32[]{:S(2)}) %collective-permute-start) | collective-permute-done | bytes 131104 | tf_op jit(solution)/shard_map/ppermute | solution.py:12
  36.1 3.5 %collective-permute-start.1 = (bf16[2,256,128]{2,1,0:T(8,128)(2,1)S(1)}, bf16[2,256,128]{2,1,0:T(8,128)(2,1)S(1)}, u32[]{:S(2)}, u32[]{:S(2)}) collective-permute-start(bf16[2,256,128]{2,1,0:T(8,128)(2,1)S(1)} %pad_maximum_fusion), channel_id=1, source_target_pairs={{0,2},{1,3},{2,4},{3,5},{4,6},{5,7},{6,8},{7,9},{8,10},{9,11},{10,... | collective-permute-start | bytes 393224 | tf_op jit(solution)/shard_map/ppermute | solution.py:12
  39.6 0.6 fusion.31
  40.2 0.5 fusion.87
  40.7 0.4 fusion.29
  41.1 0.4 fusion.95
  41.6 1.4 %collective-permute-done.1 = bf16[2,256,128]{2,1,0:T(8,128)(2,1)S(1)} collective-permute-done((bf16[2,256,128]{2,1,0:T(8,128)(2,1)S(1)}, bf16[2,256,128]{2,1,0:T(8,128)(2,1)S(1)}, u32[]{:S(2)}, u32[]{:S(2)}) %collective-permute-start.1) | collective-permute-done | bytes 131104 | tf_op jit(solution)/shard_map/ppermute | solution.py:12
  42.9 3.1 %collective-permute-start.2 = (bf16[2,256,128]{2,1,0:T(8,128)(2,1)S(1)}, bf16[2,256,128]{2,1,0:T(8,128)(2,1)S(1)}, u32[]{:S(2)}, u32[]{:S(2)}) collective-permute-start(bf16[2,256,128]{2,1,0:T(8,128)(2,1)S(1)} %pad_maximum_fusion), channel_id=1, source_target_pairs={{0,3},{1,4},{2,5},{3,6},{4,7},{5,8},{6,9},{7,10},{8,11},{9,12},{10... | collective-permute-start | bytes 393224 | tf_op jit(solution)/shard_map/ppermute | solution.py:12
  46.1 0.6 fusion.27
  46.7 0.4 fusion.86
  47.1 0.4 fusion.25
  47.6 0.4 fusion.94
  48.0 2.8 %collective-permute-done.2 = bf16[2,256,128]{2,1,0:T(8,128)(2,1)S(1)} collective-permute-done((bf16[2,256,128]{2,1,0:T(8,128)(2,1)S(1)}, bf16[2,256,128]{2,1,0:T(8,128)(2,1)S(1)}, u32[]{:S(2)}, u32[]{:S(2)}) %collective-permute-start.2) | collective-permute-done | bytes 131104 | tf_op jit(solution)/shard_map/ppermute | solution.py:12
  50.8 3.2 %collective-permute-start.15 = (bf16[2,256,128]{2,1,0:T(8,128)(2,1)S(1)}, bf16[2,256,128]{2,1,0:T(8,128)(2,1)S(1)}, u32[]{:S(2)}, u32[]{:S(2)}) collective-permute-start(bf16[2,256,128]{2,1,0:T(8,128)(2,1)S(1)} %pad_maximum_fusion.8), channel_id=1, source_target_pairs={{8,0},{9,1},{10,2},{11,3},{12,4},{13,5},{14,6},{15,7},{16,8},{17,9... | collective-permute-start | bytes 393224 | tf_op jit(solution)/shard_map/ppermute | solution.py:12
  54.0 0.6 fusion.23
  54.6 0.5 fusion.85
  55.1 0.4 fusion.21
  55.6 0.4 fusion.93
  56.0 9.6 %collective-permute-start.8 = (bf16[2,256,128]{2,1,0:T(8,128)(2,1)S(1)}, bf16[2,256,128]{2,1,0:T(8,128)(2,1)S(1)}, u32[]{:S(2)}, u32[]{:S(2)}) collective-permute-start(bf16[2,256,128]{2,1,0:T(8,128)(2,1)S(1)} %pad_maximum_fusion.1), channel_id=1, source_target_pairs={{1,0},{2,1},{3,2},{4,3},{5,4},{6,5},{7,6},{8,7},{9,8},{10,9},{11,1... | collective-permute-start | bytes 393224 | tf_op jit(solution)/shard_map/ppermute | solution.py:12
  65.7 0.6 fusion.19
  66.3 0.4 fusion.84
  66.7 0.4 fusion.17
  67.2 0.4 fusion.92
  67.6 2.5 %collective-permute-start.9 = (bf16[2,256,128]{2,1,0:T(8,128)(2,1)S(1)}, bf16[2,256,128]{2,1,0:T(8,128)(2,1)S(1)}, u32[]{:S(2)}, u32[]{:S(2)}) collective-permute-start(bf16[2,256,128]{2,1,0:T(8,128)(2,1)S(1)} %pad_maximum_fusion.2), channel_id=1, source_target_pairs={{2,0},{3,1},{4,2},{5,3},{6,4},{7,5},{8,6},{9,7},{10,8},{11,9},{12,... | collective-permute-start | bytes 393224 | tf_op jit(solution)/shard_map/ppermute | solution.py:12
  70.1 0.6 fusion.15
  70.7 0.4 fusion.83
  71.2 0.4 fusion.13
  71.6 0.4 fusion.91
  72.1 7.9 %collective-permute-start.10 = (bf16[2,256,128]{2,1,0:T(8,128)(2,1)S(1)}, bf16[2,256,128]{2,1,0:T(8,128)(2,1)S(1)}, u32[]{:S(2)}, u32[]{:S(2)}) collective-permute-start(bf16[2,256,128]{2,1,0:T(8,128)(2,1)S(1)} %pad_maximum_fusion.3), channel_id=1, source_target_pairs={{3,0},{4,1},{5,2},{6,3},{7,4},{8,5},{9,6},{10,7},{11,8},{12,9},{13... | collective-permute-start | bytes 393224 | tf_op jit(solution)/shard_map/ppermute | solution.py:12
  80.0 0.6 fusion.11
  80.7 0.4 fusion.82
  81.1 0.4 fusion.9
  81.6 0.4 fusion.90
  82.0 1.9 %collective-permute-start.11 = (bf16[2,256,128]{2,1,0:T(8,128)(2,1)S(1)}, bf16[2,256,128]{2,1,0:T(8,128)(2,1)S(1)}, u32[]{:S(2)}, u32[]{:S(2)}) collective-permute-start(bf16[2,256,128]{2,1,0:T(8,128)(2,1)S(1)} %pad_maximum_fusion.4), channel_id=1, source_target_pairs={{4,0},{5,1},{6,2},{7,3},{8,4},{9,5},{10,6},{11,7},{12,8},{13,9},{1... | collective-permute-start | bytes 393224 | tf_op jit(solution)/shard_map/ppermute | solution.py:12
  83.9 0.6 fusion.7
  84.6 0.5 fusion.81
  85.0 0.5 fusion.5
  85.5 0.4 fusion.89
  88.4 3.4 %collective-permute-start.12 = (bf16[2,256,128]{2,1,0:T(8,128)(2,1)S(1)}, bf16[2,256,128]{2,1,0:T(8,128)(2,1)S(1)}, u32[]{:S(2)}, u32[]{:S(2)}) collective-permute-start(bf16[2,256,128]{2,1,0:T(8,128)(2,1)S(1)} %pad_maximum_fusion.5), channel_id=1, source_target_pairs={{5,0},{6,1},{7,2},{8,3},{9,4},{10,5},{11,6},{12,7},{13,8},{14,9},{... | collective-permute-start | bytes 393224 | tf_op jit(solution)/shard_map/ppermute | solution.py:12
  91.9 11.5 %collective-permute-start.13 = (bf16[2,256,128]{2,1,0:T(8,128)(2,1)S(1)}, bf16[2,256,128]{2,1,0:T(8,128)(2,1)S(1)}, u32[]{:S(2)}, u32[]{:S(2)}) collective-permute-start(bf16[2,256,128]{2,1,0:T(8,128)(2,1)S(1)} %pad_maximum_fusion.6), channel_id=1, source_target_pairs={{6,0},{7,1},{8,2},{9,3},{10,4},{11,5},{12,6},{13,7},{14,8},{15,9},... | collective-permute-start | bytes 393224 | tf_op jit(solution)/shard_map/ppermute | solution.py:12
  103.4 2.7 %collective-permute-start.14 = (bf16[2,256,128]{2,1,0:T(8,128)(2,1)S(1)}, bf16[2,256,128]{2,1,0:T(8,128)(2,1)S(1)}, u32[]{:S(2)}, u32[]{:S(2)}) collective-permute-start(bf16[2,256,128]{2,1,0:T(8,128)(2,1)S(1)} %pad_maximum_fusion.7), channel_id=1, source_target_pairs={{7,0},{8,1},{9,2},{10,3},{11,4},{12,5},{13,6},{14,7},{15,8},{16,9}... | collective-permute-start | bytes 393224 | tf_op jit(solution)/shard_map/ppermute | solution.py:12
  106.4 1.0 copy.235
  107.4 6.5 %collective-permute-done.14 = bf16[2,256,128]{2,1,0:T(8,128)(2,1)S(1)} collective-permute-done((bf16[2,256,128]{2,1,0:T(8,128)(2,1)S(1)}, bf16[2,256,128]{2,1,0:T(8,128)(2,1)S(1)}, u32[]{:S(2)}, u32[]{:S(2)}) %collective-permute-start.14) | collective-permute-done | bytes 131104 | tf_op jit(solution)/shard_map/ppermute | solution.py:12
  114.1 0.7 slice_bitcast_fusion
  (56 shorter events, 4.7 us)
Async XLA Ops:
  0.6 25.9 %copy-start = (bf16[256,1024]{1,0:T(8,128)(2,1)S(1)}, bf16[256,1024]{1,0:T(8,128)(2,1)}, u32[]{:S(2)}) copy-start(bf16[256,1024]{1,0:T(8,128)(2,1)} %param.7) | copy-start | bytes 1572868
  1.6 28.2 %collective-permute-start.7 = (bf16[2,256,128]{2,1,0:T(8,128)(2,1)S(1)}, bf16[2,256,128]{2,1,0:T(8,128)(2,1)S(1)}, u32[]{:S(2)}, u32[]{:S(2)}) collective-permute-start(bf16[2,256,128]{2,1,0:T(8,128)(2,1)S(1)} %pad_maximum_fusion), channel_id=1, source_target_pairs={{0,8},{1,9},{2,10},{3,11},{4,12},{5,13},{6,14},{7,15},{8,16},{9,17... | collective-permute-start | bytes 393224 | tf_op jit(solution)/shard_map/ppermute | solution.py:12
  5.4 76.6 %collective-permute-start.6 = (bf16[2,256,128]{2,1,0:T(8,128)(2,1)S(1)}, bf16[2,256,128]{2,1,0:T(8,128)(2,1)S(1)}, u32[]{:S(2)}, u32[]{:S(2)}) collective-permute-start(bf16[2,256,128]{2,1,0:T(8,128)(2,1)S(1)} %pad_maximum_fusion), channel_id=1, source_target_pairs={{0,7},{1,8},{2,9},{3,10},{4,11},{5,12},{6,13},{7,14},{8,15},{9,16}... | collective-permute-start | bytes 393224 | tf_op jit(solution)/shard_map/ppermute | solution.py:12
  8.5 63.6 %collective-permute-start.5 = (bf16[2,256,128]{2,1,0:T(8,128)(2,1)S(1)}, bf16[2,256,128]{2,1,0:T(8,128)(2,1)S(1)}, u32[]{:S(2)}, u32[]{:S(2)}) collective-permute-start(bf16[2,256,128]{2,1,0:T(8,128)(2,1)S(1)} %pad_maximum_fusion), channel_id=1, source_target_pairs={{0,6},{1,7},{2,8},{3,9},{4,10},{5,11},{6,12},{7,13},{8,14},{9,15},... | collective-permute-start | bytes 393224 | tf_op jit(solution)/shard_map/ppermute | solution.py:12
  12.1 55.5 %collective-permute-start.4 = (bf16[2,256,128]{2,1,0:T(8,128)(2,1)S(1)}, bf16[2,256,128]{2,1,0:T(8,128)(2,1)S(1)}, u32[]{:S(2)}, u32[]{:S(2)}) collective-permute-start(bf16[2,256,128]{2,1,0:T(8,128)(2,1)S(1)} %pad_maximum_fusion), channel_id=1, source_target_pairs={{0,5},{1,6},{2,7},{3,8},{4,9},{5,10},{6,11},{7,12},{8,13},{9,14},{... | collective-permute-start | bytes 393224 | tf_op jit(solution)/shard_map/ppermute | solution.py:12
  17.3 38.7 %collective-permute-start.3 = (bf16[2,256,128]{2,1,0:T(8,128)(2,1)S(1)}, bf16[2,256,128]{2,1,0:T(8,128)(2,1)S(1)}, u32[]{:S(2)}, u32[]{:S(2)}) collective-permute-start(bf16[2,256,128]{2,1,0:T(8,128)(2,1)S(1)} %pad_maximum_fusion), channel_id=1, source_target_pairs={{0,4},{1,5},{2,6},{3,7},{4,8},{5,9},{6,10},{7,11},{8,12},{9,13},{1... | collective-permute-start | bytes 393224 | tf_op jit(solution)/shard_map/ppermute | solution.py:12
  24.8 1.7 %copy-start.3 = (bf16[256,128]{1,0:T(8,128)(2,1)S(1)}, bf16[256,128]{1,0:T(8,128)(2,1)}, u32[]{:S(2)}) copy-start(bf16[256,128]{1,0:T(8,128)(2,1)} %param.8) | copy-start | bytes 196612
  24.8 1.7 %copy-start.4 = (f32[8,256]{1,0:T(8,128)S(1)}, f32[8,256]{1,0:T(8,128)}, u32[]{:S(2)}) copy-start(f32[8,256]{1,0:T(8,128)} %param.12) | copy-start | bytes 24580
  25.4 1.7 %copy-start.1 = (bf16[256,1024]{1,0:T(8,128)(2,1)S(1)}, bf16[256,1024]{1,0:T(8,128)(2,1)}, u32[]{:S(2)}) copy-start(bf16[256,1024]{1,0:T(8,128)(2,1)} %param.11) | copy-start | bytes 1572868
  27.1 0.8 copy-start.2
  29.8 6.3 %collective-permute-start = (bf16[2,256,128]{2,1,0:T(8,128)(2,1)S(1)}, bf16[2,256,128]{2,1,0:T(8,128)(2,1)S(1)}, u32[]{:S(2)}, u32[]{:S(2)}) collective-permute-start(bf16[2,256,128]{2,1,0:T(8,128)(2,1)S(1)} %pad_maximum_fusion), channel_id=1, source_target_pairs={{0,1},{1,2},{2,3},{3,4},{4,5},{5,6},{6,7},{7,8},{8,9},{9,10},{10,1... | collective-permute-start | bytes 393224 | tf_op jit(solution)/shard_map/ppermute | solution.py:12
  36.1 6.8 %collective-permute-start.1 = (bf16[2,256,128]{2,1,0:T(8,128)(2,1)S(1)}, bf16[2,256,128]{2,1,0:T(8,128)(2,1)S(1)}, u32[]{:S(2)}, u32[]{:S(2)}) collective-permute-start(bf16[2,256,128]{2,1,0:T(8,128)(2,1)S(1)} %pad_maximum_fusion), channel_id=1, source_target_pairs={{0,2},{1,3},{2,4},{3,5},{4,6},{5,7},{6,8},{7,9},{8,10},{9,11},{10,... | collective-permute-start | bytes 393224 | tf_op jit(solution)/shard_map/ppermute | solution.py:12
  42.9 7.9 %collective-permute-start.2 = (bf16[2,256,128]{2,1,0:T(8,128)(2,1)S(1)}, bf16[2,256,128]{2,1,0:T(8,128)(2,1)S(1)}, u32[]{:S(2)}, u32[]{:S(2)}) collective-permute-start(bf16[2,256,128]{2,1,0:T(8,128)(2,1)S(1)} %pad_maximum_fusion), channel_id=1, source_target_pairs={{0,3},{1,4},{2,5},{3,6},{4,7},{5,8},{6,9},{7,10},{8,11},{9,12},{10... | collective-permute-start | bytes 393224 | tf_op jit(solution)/shard_map/ppermute | solution.py:12
  50.8 37.6 %collective-permute-start.15 = (bf16[2,256,128]{2,1,0:T(8,128)(2,1)S(1)}, bf16[2,256,128]{2,1,0:T(8,128)(2,1)S(1)}, u32[]{:S(2)}, u32[]{:S(2)}) collective-permute-start(bf16[2,256,128]{2,1,0:T(8,128)(2,1)S(1)} %pad_maximum_fusion.8), channel_id=1, source_target_pairs={{8,0},{9,1},{10,2},{11,3},{12,4},{13,5},{14,6},{15,7},{16,8},{17,9... | collective-permute-start | bytes 393224 | tf_op jit(solution)/shard_map/ppermute | solution.py:12
  56.0 35.8 %collective-permute-start.8 = (bf16[2,256,128]{2,1,0:T(8,128)(2,1)S(1)}, bf16[2,256,128]{2,1,0:T(8,128)(2,1)S(1)}, u32[]{:S(2)}, u32[]{:S(2)}) collective-permute-start(bf16[2,256,128]{2,1,0:T(8,128)(2,1)S(1)} %pad_maximum_fusion.1), channel_id=1, source_target_pairs={{1,0},{2,1},{3,2},{4,3},{5,4},{6,5},{7,6},{8,7},{9,8},{10,9},{11,1... | collective-permute-start | bytes 393224 | tf_op jit(solution)/shard_map/ppermute | solution.py:12
  67.6 35.7 %collective-permute-start.9 = (bf16[2,256,128]{2,1,0:T(8,128)(2,1)S(1)}, bf16[2,256,128]{2,1,0:T(8,128)(2,1)S(1)}, u32[]{:S(2)}, u32[]{:S(2)}) collective-permute-start(bf16[2,256,128]{2,1,0:T(8,128)(2,1)S(1)} %pad_maximum_fusion.2), channel_id=1, source_target_pairs={{2,0},{3,1},{4,2},{5,3},{6,4},{7,5},{8,6},{9,7},{10,8},{11,9},{12,... | collective-permute-start | bytes 393224 | tf_op jit(solution)/shard_map/ppermute | solution.py:12
  72.1 35.3 %collective-permute-start.10 = (bf16[2,256,128]{2,1,0:T(8,128)(2,1)S(1)}, bf16[2,256,128]{2,1,0:T(8,128)(2,1)S(1)}, u32[]{:S(2)}, u32[]{:S(2)}) collective-permute-start(bf16[2,256,128]{2,1,0:T(8,128)(2,1)S(1)} %pad_maximum_fusion.3), channel_id=1, source_target_pairs={{3,0},{4,1},{5,2},{6,3},{7,4},{8,5},{9,6},{10,7},{11,8},{12,9},{13... | collective-permute-start | bytes 393224 | tf_op jit(solution)/shard_map/ppermute | solution.py:12
  82.0 25.4 %collective-permute-start.11 = (bf16[2,256,128]{2,1,0:T(8,128)(2,1)S(1)}, bf16[2,256,128]{2,1,0:T(8,128)(2,1)S(1)}, u32[]{:S(2)}, u32[]{:S(2)}) collective-permute-start(bf16[2,256,128]{2,1,0:T(8,128)(2,1)S(1)} %pad_maximum_fusion.4), channel_id=1, source_target_pairs={{4,0},{5,1},{6,2},{7,3},{8,4},{9,5},{10,6},{11,7},{12,8},{13,9},{1... | collective-permute-start | bytes 393224 | tf_op jit(solution)/shard_map/ppermute | solution.py:12
  88.4 19.0 %collective-permute-start.12 = (bf16[2,256,128]{2,1,0:T(8,128)(2,1)S(1)}, bf16[2,256,128]{2,1,0:T(8,128)(2,1)S(1)}, u32[]{:S(2)}, u32[]{:S(2)}) collective-permute-start(bf16[2,256,128]{2,1,0:T(8,128)(2,1)S(1)} %pad_maximum_fusion.5), channel_id=1, source_target_pairs={{5,0},{6,1},{7,2},{8,3},{9,4},{10,5},{11,6},{12,7},{13,8},{14,9},{... | collective-permute-start | bytes 393224 | tf_op jit(solution)/shard_map/ppermute | solution.py:12
  91.9 15.5 %collective-permute-start.13 = (bf16[2,256,128]{2,1,0:T(8,128)(2,1)S(1)}, bf16[2,256,128]{2,1,0:T(8,128)(2,1)S(1)}, u32[]{:S(2)}, u32[]{:S(2)}) collective-permute-start(bf16[2,256,128]{2,1,0:T(8,128)(2,1)S(1)} %pad_maximum_fusion.6), channel_id=1, source_target_pairs={{6,0},{7,1},{8,2},{9,3},{10,4},{11,5},{12,6},{13,7},{14,8},{15,9},... | collective-permute-start | bytes 393224 | tf_op jit(solution)/shard_map/ppermute | solution.py:12
  103.4 10.6 %collective-permute-start.14 = (bf16[2,256,128]{2,1,0:T(8,128)(2,1)S(1)}, bf16[2,256,128]{2,1,0:T(8,128)(2,1)S(1)}, u32[]{:S(2)}, u32[]{:S(2)}) collective-permute-start(bf16[2,256,128]{2,1,0:T(8,128)(2,1)S(1)} %pad_maximum_fusion.7), channel_id=1, source_target_pairs={{7,0},{8,1},{9,2},{10,3},{11,4},{12,5},{13,6},{14,7},{15,8},{16,9}... | collective-permute-start | bytes 393224 | tf_op jit(solution)/shard_map/ppermute | solution.py:12
where the time goes:
time: 115 us
  starting transfers between devices  71.1 us (62%)
  matrix products  20.5 us (18%)
  waiting for transfers between devices  13 us (11%)
  other arithmetic  4.51 us (4%)
  local copies, waits for them, and re-layouts  4.19 us (4%)
  between operations  1.38 us (1%)
    ppermute x16, starting transfers between devices, passed_along(): lax.ppermute(value, axis, [(source, source + steps) for source in range(i...  71.1 us
    ppermute x16, waiting for transfers between devices, passed_along(): lax.ppermute(value, axis, [(source, source + steps) for source in range(i...  13 us
    dot_general x9, matrix products, pair_terms(): jnp.einsum('qhd,kd->hqk', q_heads, kblock, preferred_element_type=jnp.flo...  5.53 us
    dot_general x9, matrix products, pair_terms(): jnp.einsum('hqk,qhd->kd', prob_low, g_heads, preferred_element_type=jnp.f...  4.11 us
    dot_general x9, matrix products, pair_terms(): jnp.einsum('qhd,kd->hqk', g_heads, vblock, preferred_element_type=jnp.flo...  4.01 us
    dot_general x9, matrix products, pair_terms(): jnp.einsum('hqk,qhd->kd', dscore, q_heads, preferred_element_type=jnp.flo...  3.87 us
    dot_general x9, matrix products, pair_terms(): jnp.einsum('hqk,kd->qhd', dscore, kblock, preferred_element_type=jnp.floa...  3.02 us
    unnamed x13, local copies, waits for them, and re-layouts  2.74 us
  transfers between devices with their start and end apart: 16, of which 4 were waited for; matrix products, arithmetic and copies ran while one was open for 24% of the time, Pallas kernels for 0%

commit v1 on v0

v1 whole, which is shorter than its diff:
```python
import functools
import math

import jax
import jax.numpy as jnp
from jax import lax
from jax.experimental import pallas as pl
from jax.experimental.pallas import tpu as pltpu
from jax.sharding import PartitionSpec as P

MESH = pl.DeviceIdType.MESH
F32 = jnp.float32
BF16 = jnp.bfloat16
HEADS = 8
DIM = 128
TOK = 256
REACH = 4


def nn(a, b):
    return lax.dot_general(a, b, (((1,), (0,)), ((), ())), preferred_element_type=F32)


def nt(a, b):
    return lax.dot_general(a, b, (((1,), (1,)), ((), ())), preferred_element_type=F32)


def kernel(
    outer, inner, q_hbm, k_hbm, v_hbm, o_hbm, g_hbm, lse_hbm, docs, dq_hbm, dk_out, dv_out,
    qs, gs, os, rows, kv, kt, bias, start, probs, ds, acc, own, ret_out, ret_in, dq_out, dq_in, dq_fin,
    load_sem, kv_send, kv_recv, ret_send, ret_recv, sib_send, sib_recv, store_sem,
):
    dp = lax.axis_index("dp")
    here = lax.axis_index("outer") * inner + lax.axis_index("inner")
    core = lax.rem(here, 2)
    total = outer * inner
    scale = 1.0 / DIM**0.5
    log2e = math.log2(math.e)

    def device(index):
        index = lax.rem(index + total, total)
        return (dp, index // inner, lax.rem(index, inner))

    sibling = device(here + 1 - 2 * core)

    loads = []

    def load(src, dst, n):
        copy = pltpu.make_async_copy(src, dst, load_sem.at[n])
        copy.start()
        loads.append(copy)

    load(k_hbm, kv.at[0, pl.ds(0, TOK)], 0)
    load(v_hbm, kv.at[0, pl.ds(TOK, TOK)], 1)
    for h in range(HEADS):
        load(q_hbm.at[:, pl.ds(h * DIM, DIM)], qs.at[0, pl.ds(h * TOK, TOK)], 2 + h)
        load(g_hbm.at[:, pl.ds(h * DIM, DIM)], gs.at[0, pl.ds(h * TOK, TOK)], 10 + h)
        load(o_hbm.at[:, pl.ds(h * DIM, DIM)], os.at[pl.ds(h * TOK, TOK)], 18 + h)
    load(lse_hbm, rows.at[0, pl.ds(0, HEADS)], 26)

    barrier = pltpu.get_barrier_semaphore()
    pl.semaphore_signal(barrier, inc=1, device_id=sibling, device_id_type=MESH)
    for k in range(1, REACH + 1):
        for way in (1, -1):
            pl.semaphore_signal(barrier, inc=1, device_id=device(here + way * 2 * k), device_id_type=MESH)

    lane = lax.broadcasted_iota(jnp.int32, (8, TOK), 1)
    first = here * TOK
    other = (here + 1 - 2 * core) * TOK
    end = jnp.int32(0)
    low = [jnp.zeros((8, TOK), jnp.int32) for _ in range(2)]
    for d in range(docs.shape[0]):
        end = end + docs[d]
        low = [
            jnp.where(lane + base >= end, end, x) for base, x in zip((first, other), low)
        ]
    start[0] = low[0]
    start[1] = low[1]

    pl.semaphore_wait(barrier, 2 * REACH + 1)
    for copy in loads[:2]:
        copy.wait()

    def kv_copy(k):
        return pltpu.make_async_remote_copy(
            src_ref=kv.at[0], dst_ref=kv.at[k], send_sem=kv_send.at[k], recv_sem=kv_recv.at[k],
            device_id=device(here + 2 * k), device_id_type=MESH,
        )

    def ret_copy(k):
        return pltpu.make_async_remote_copy(
            src_ref=ret_out.at[k], dst_ref=ret_in.at[k], send_sem=ret_send.at[k], recv_sem=ret_recv.at[k],
            device_id=device(here - 2 * k), device_id_type=MESH,
        )

    def sib_copy(src, dst, n):
        return pltpu.make_async_remote_copy(
            src_ref=src, dst_ref=dst, send_sem=sib_send.at[n], recv_sem=sib_recv.at[n],
            device_id=sibling, device_id_type=MESH,
        )

    for k in range(1, REACH + 1):
        kv_copy(k).start()
    for copy in loads[2:]:
        copy.wait()
    to_sib = [sib_copy(qs.at[0], qs.at[1], 0), sib_copy(gs.at[0], gs.at[1], 1)]
    for copy in to_sib:
        copy.start()

    row = lax.broadcasted_iota(jnp.int32, (HEADS, DIM), 0)
    delta = jnp.zeros((HEADS, TOK), F32)
    for h in range(HEADS):
        part = pl.ds(h * TOK, TOK)
        prod = gs[0, part, :].astype(F32) * os[part, :].astype(F32)
        hi = prod.astype(BF16)
        lo = (prod - hi.astype(F32)).astype(BF16)
        pick = jnp.where(row == h, 1.0, 0.0).astype(BF16)
        delta = delta + (nt(pick, hi) + nt(pick, lo))
    rows[0, HEADS:, :] = delta
    rows[0, :HEADS, :] = rows[0, :HEADS, :] * log2e
    to_sib.append(sib_copy(rows.at[0], rows.at[1], 2))
    to_sib[2].start()

    def pair(k, a):
        query_base = lax.select(a == 0, first, other)
        key_base = (here - 2 * k) * TOK
        t = key_base + lax.broadcasted_iota(jnp.int32, (TOK, TOK), 0)
        p = query_base + lax.broadcasted_iota(jnp.int32, (TOK, TOK), 1)
        ok = (t >= start[a, 0:1, :]) & (t <= p)
        bias[...] = jnp.where(ok, 0.0, -jnp.inf)
        keys = kv[k, :TOK, :]
        values = kv[k, TOK:, :]
        for h in range(HEADS):
            part = pl.ds(h * TOK, TOK)
            scores = nt(keys, qs[a, part, :])
            dprob = nt(values, gs[a, part, :])
            prob = jnp.exp2(scores * (scale * log2e) - rows[a, h : h + 1, :] + bias[...])
            dscore = prob * (dprob - rows[a, HEADS + h : HEADS + h + 1, :])
            probs[:, h * TOK : (h + 1) * TOK] = prob.astype(BF16)
            ds[a, k, :, h * TOK : (h + 1) * TOK] = dscore.astype(BF16)
        acc[:TOK, :] += nn(ds[a, k], qs[a])
        acc[TOK:, :] += nn(probs[...], gs[a])

    def block(k, _):
        @pl.when(k > 0)
        def _():
            kv_copy(k).wait_recv()

        kt[k] = kv[k, :TOK, :].T
        acc[...] = jnp.zeros_like(acc)
        pair(k, 0)

        @pl.when(k == core)
        def _():
            for copy in to_sib:
                copy.wait_recv()

        @pl.when((k >= core) & (k < core + REACH))
        def _():
            pair(k, 1)

        acc[:TOK, :] = acc[:TOK, :] * scale

        @pl.when(k == 0)
        def _():
            own[...] = acc[...]

        @pl.when(k > 0)
        def _():
            ret_out[k] = acc[...].astype(BF16)
            ret_copy(k).start()

        return 0

    lax.fori_loop(0, REACH + 1, block, 0)

    for h in range(HEADS):
        cols = pl.ds(h * TOK, TOK)
        part = sum(nn(kt[core + m], ds[1, core + m, :, cols]) for m in range(REACH))
        dq_out[h] = (part * scale).astype(BF16)
    dq_copy = sib_copy(dq_out, dq_in, 3)
    dq_copy.start()
    for copy in to_sib:
        copy.wait_send()
    dq_copy.wait_recv()
    for h in range(HEADS):
        cols = pl.ds(h * TOK, TOK)
        part = sum(nn(kt[m], ds[0, m, :, cols]) for m in range(REACH + 1))
        both = part * scale + dq_in[h].astype(F32)
        dq_fin[:, h * DIM : (h + 1) * DIM] = both.T.astype(BF16)
    store = pltpu.make_async_copy(dq_fin, dq_hbm, store_sem)
    store.start()

    grads = own[...]
    for k in range(1, REACH + 1):
        ret_copy(k).wait_recv()
        grads = grads + ret_in[k].astype(F32)
    dk_out[...] = grads[:TOK].astype(BF16)
    dv_out[...] = grads[TOK:].astype(BF16)

    dq_copy.wait_send()
    for k in range(1, REACH + 1):
        kv_copy(k).wait_send()
        ret_copy(k).wait_send()
    store.wait()


def local(outer, inner, queries, keys, values, outputs, out_grads, log_sums, doc_lengths):
    wide = HEADS * TOK
    anywhere = pl.BlockSpec(memory_space=pl.ANY)
    vmem = pl.BlockSpec(memory_space=pltpu.VMEM)
    dma = pltpu.SemaphoreType.DMA
    return pl.pallas_call(
        functools.partial(kernel, outer, inner),
        out_shape=[
            jax.ShapeDtypeStruct((TOK, HEADS * DIM), BF16),
            jax.ShapeDtypeStruct((TOK, DIM), BF16),
            jax.ShapeDtypeStruct((TOK, DIM), BF16),
        ],
        in_specs=[anywhere] * 6 + [pl.BlockSpec(memory_space=pltpu.SMEM)],
        out_specs=[anywhere, vmem, vmem],
        scratch_shapes=[
            pltpu.VMEM((2, wide, DIM), BF16),
            pltpu.VMEM((2, wide, DIM), BF16),
            pltpu.VMEM((wide, DIM), BF16),
            pltpu.VMEM((2, 2 * HEADS, TOK), F32),
            pltpu.VMEM((REACH + 1, 2 * TOK, DIM), BF16),
            pltpu.VMEM((REACH + 1, DIM, TOK), BF16),
            pltpu.VMEM((TOK, TOK), F32),
            pltpu.VMEM((2, 8, TOK), jnp.int32),
            pltpu.VMEM((TOK, wide), BF16),
            pltpu.VMEM((2, REACH + 1, TOK, wide), BF16),
            pltpu.VMEM((2 * TOK, DIM), F32),
            pltpu.VMEM((2 * TOK, DIM), F32),
            pltpu.VMEM((REACH + 1, 2 * TOK, DIM), BF16),
            pltpu.VMEM((REACH + 1, 2 * TOK, DIM), BF16),
            pltpu.VMEM((HEADS, DIM, TOK), BF16),
            pltpu.VMEM((HEADS, DIM, TOK), BF16),
            pltpu.VMEM((TOK, HEADS * DIM), BF16),
            dma((27,)),
            dma((REACH + 1,)),
            dma((REACH + 1,)),
            dma((REACH + 1,)),
            dma((REACH + 1,)),
            dma((4,)),
            dma((4,)),
            dma,
        ],
        compiler_params=pltpu.CompilerParams(
            collective_id=0, has_side_effects=True, vmem_limit_bytes=48 << 20
        ),
        name="attention_backward",
    )(queries, keys, values, outputs, out_grads, log_sums, doc_lengths)


def solution(mesh):
    rows = P(("dp", "outer", "inner"), None)
    return jax.shard_map(
        functools.partial(local, mesh.shape["outer"], mesh.shape["inner"]),
        mesh=mesh,
        in_specs=(rows,) * 5 + (P(None, ("dp", "outer", "inner")), P("dp")),
        out_specs=(rows,) * 3,
        check_vma=False,
    )
```

time: 115 us -> 43.5 us (0.38)
  the two profiles are of different devices: /device:TPU:182 before, /device:TPU:8 now
where the time goes in v1:
time: 43.5 us; the launch traced here: 43.1 us
  Pallas kernels  34.3 us (79%)
  local copies, waits for them, and re-layouts  8.2 us (19%)
  between operations  0.66 us (2%)
    pallas_call x1, Pallas kernels, local(): pl.pallas_call(functools.partial(kernel, outer, inner), out_shape=[jax.Sh...  34.3 us
    unnamed x17, local copies, waits for them, and re-layouts  8.2 us

profile of v1, /device:TPU:8, one launch (start us, length us, event | category | flops | bytes accessed | tf_op | source)
XLA Modules:
  0.0 43.1 jit_solution(6880774288364561979)
XLA Ops:
  0.6 0.0 copy-start
  0.6 1.0 %copy-done = bf16[256,1024]{1,0:T(8,128)(2,1)S(1)} copy-done((bf16[256,1024]{1,0:T(8,128)(2,1)S(1)}, bf16[256,1024]{1,0:T(8,128)(2,1)}, u32[]{:S(2)}) %copy-start) | copy-done | bytes 524312
  1.7 0.0 copy-start.1
  1.7 1.0 %copy-done.1 = bf16[256,1024]{1,0:T(8,128)(2,1)S(1)} copy-done((bf16[256,1024]{1,0:T(8,128)(2,1)S(1)}, bf16[256,1024]{1,0:T(8,128)(2,1)}, u32[]{:S(2)}) %copy-start.1) | copy-done | bytes 524312
  2.7 0.0 copy-start.2
  2.7 1.0 %copy-done.2 = bf16[256,1024]{1,0:T(8,128)(2,1)S(1)} copy-done((bf16[256,1024]{1,0:T(8,128)(2,1)S(1)}, bf16[256,1024]{1,0:T(8,128)(2,1)}, u32[]{:S(2)}) %copy-start.2) | copy-done | bytes 524312
  3.8 0.0 copy-start.3
  3.8 0.8 %copy-done.3 = bf16[256,128]{1,0:T(8,128)(2,1)S(1)} copy-done((bf16[256,128]{1,0:T(8,128)(2,1)S(1)}, bf16[256,128]{1,0:T(8,128)(2,1)}, u32[]{:S(2)}) %copy-start.3) | copy-done | bytes 65560
  4.6 0.0 copy-start.4
  4.6 0.8 %copy-done.4 = bf16[256,128]{1,0:T(8,128)(2,1)S(1)} copy-done((bf16[256,128]{1,0:T(8,128)(2,1)S(1)}, bf16[256,128]{1,0:T(8,128)(2,1)}, u32[]{:S(2)}) %copy-start.4) | copy-done | bytes 65560
  5.4 0.0 copy-start.5
  5.4 0.7 %copy-done.5 = f32[8,256]{1,0:T(8,128)S(1)} copy-done((f32[8,256]{1,0:T(8,128)S(1)}, f32[8,256]{1,0:T(8,128)}, u32[]{:S(2)}) %copy-start.5) | copy-done | bytes 8216
  6.1 0.0 copy-start.6
  6.1 0.7 %copy-done.6 = s32[32]{0:T(128)S(1)} copy-done((s32[32]{0:T(128)S(1)}, s32[32]{0:T(128)}, u32[]{:S(2)}) %copy-start.6) | copy-done | bytes 152
  6.8 34.3 %attention_backward.1 = (bf16[256,1024]{1,0:T(8,128)(2,1)S(1)}, bf16[256,128]{1,0:T(8,128)(2,1)S(1)}, bf16[256,128]{1,0:T(8,128)(2,1)S(1)}) custom-call(bf16[256,1024]{1,0:T(8,128)(2,1)S(1)} %copy-done, bf16[256,128]{1,0:T(8,128)(2,1)S(1)} %copy-done.3, bf16[256,128]{1,0:T(8,128)(2,1)S(1)} %copy-done.4, bf16[256,1024]{1,0:T(8,128)(2,1)S(1)} %copy-done.1, ...), custom_call_target="tpu_custom_call" | custom-call | tf_op jit(solution)/shard_map/attention_backward/pallas_call | solution.py:213
  41.1 0.8 %copy.13 = bf16[256,1024]{1,0:T(8,128)(2,1)} copy(bf16[256,1024]{1,0:T(8,128)(2,1)S(1)} %get-tuple-element.6) | data formatting | bytes 1048576
  41.9 0.6 %copy.14 = bf16[256,128]{1,0:T(8,128)(2,1)} copy(bf16[256,128]{1,0:T(8,128)(2,1)S(1)} %get-tuple-element.7) | data formatting | bytes 131072
  42.5 0.6 %copy.15 = bf16[256,128]{1,0:T(8,128)(2,1)} copy(bf16[256,128]{1,0:T(8,128)(2,1)S(1)} %get-tuple-element.8) | data formatting | bytes 131072
Async XLA Ops:
  0.6 1.0 %copy-start = (bf16[256,1024]{1,0:T(8,128)(2,1)S(1)}, bf16[256,1024]{1,0:T(8,128)(2,1)}, u32[]{:S(2)}) copy-start(bf16[256,1024]{1,0:T(8,128)(2,1)} %q_hbm.1) | copy-start | bytes 1572868
  1.7 1.0 %copy-start.1 = (bf16[256,1024]{1,0:T(8,128)(2,1)S(1)}, bf16[256,1024]{1,0:T(8,128)(2,1)}, u32[]{:S(2)}) copy-start(bf16[256,1024]{1,0:T(8,128)(2,1)} %o_hbm.1) | copy-start | bytes 1572868
  2.7 1.0 %copy-start.2 = (bf16[256,1024]{1,0:T(8,128)(2,1)S(1)}, bf16[256,1024]{1,0:T(8,128)(2,1)}, u32[]{:S(2)}) copy-start(bf16[256,1024]{1,0:T(8,128)(2,1)} %g_hbm.1) | copy-start | bytes 1572868
  3.8 0.8 %copy-start.3 = (bf16[256,128]{1,0:T(8,128)(2,1)S(1)}, bf16[256,128]{1,0:T(8,128)(2,1)}, u32[]{:S(2)}) copy-start(bf16[256,128]{1,0:T(8,128)(2,1)} %k_hbm.1) | copy-start | bytes 196612
  4.6 0.8 %copy-start.4 = (bf16[256,128]{1,0:T(8,128)(2,1)S(1)}, bf16[256,128]{1,0:T(8,128)(2,1)}, u32[]{:S(2)}) copy-start(bf16[256,128]{1,0:T(8,128)(2,1)} %v_hbm.1) | copy-start | bytes 196612
  5.4 0.7 %copy-start.5 = (f32[8,256]{1,0:T(8,128)S(1)}, f32[8,256]{1,0:T(8,128)}, u32[]{:S(2)}) copy-start(f32[8,256]{1,0:T(8,128)} %lse_hbm.1) | copy-start | bytes 24580
  6.1 0.7 %copy-start.6 = (s32[32]{0:T(128)S(1)}, s32[32]{0:T(128)}, u32[]{:S(2)}) copy-start(s32[32]{0:T(128)} %docs.1) | copy-start | bytes 388

commit v2 on v1

--- a/solution.py
+++ b/solution.py
@@ -26,8 +26,8 @@
 
 
 def kernel(
-    outer, inner, q_hbm, k_hbm, v_hbm, o_hbm, g_hbm, lse_hbm, docs, dq_hbm, dk_out, dv_out,
-    qs, gs, os, rows, kv, kt, bias, start, probs, ds, acc, own, ret_out, ret_in, dq_out, dq_in, dq_fin,
+    outer, inner, q_hbm, k_hbm, v_hbm, o_hbm, g_hbm, lse_hbm, docs, dq_hbm, dk_hbm, dv_hbm,
+    qs, gs, os, rows, kv, kt, bias, start, probs, ds, acc, own, ret_out, ret_in, dq_out, dq_in, dq_fin, dkv_fin,
     load_sem, kv_send, kv_recv, ret_send, ret_recv, sib_send, sib_recv, store_sem,
 ):
     dp = lax.axis_index("dp")
@@ -43,6 +43,23 @@
 
     sibling = device(here + 1 - 2 * core)
 
+    def ahead(k):
+        return here + 2 * k < total
+
+    def behind(k):
+        return here - 2 * k >= 0
+
+    barrier = pltpu.get_barrier_semaphore()
+    pl.semaphore_signal(barrier, inc=1, device_id=sibling, device_id_type=MESH)
+    for k in range(1, REACH + 1):
+        for reaches, way in ((ahead, 1), (behind, -1)):
+
+            @pl.when(reaches(k))
+            def _():
+                pl.semaphore_signal(
+                    barrier, inc=1, device_id=device(here + way * 2 * k), device_id_type=MESH
+                )
+
     loads = []
 
     def load(src, dst, n):
@@ -58,11 +75,40 @@
         load(o_hbm.at[:, pl.ds(h * DIM, DIM)], os.at[pl.ds(h * TOK, TOK)], 18 + h)
     load(lse_hbm, rows.at[0, pl.ds(0, HEADS)], 26)
 
-    barrier = pltpu.get_barrier_semaphore()
-    pl.semaphore_signal(barrier, inc=1, device_id=sibling, device_id_type=MESH)
-    for k in range(1, REACH + 1):
-        for way in (1, -1):
-            pl.semaphore_signal(barrier, inc=1, device_id=device(here + way * 2 * k), device_id_type=MESH)
+    greeted = jnp.int32(1)
+    for k in range(1, REACH + 1):
+        for reaches in (ahead, behind):
+            greeted = greeted + jnp.where(reaches(k), 1, 0)
+    pl.semaphore_wait(barrier, greeted)
+    for copy in loads[:2]:
+        copy.wait()
+
+    def kv_copy(k):
+        return pltpu.make_async_remote_copy(
+            src_ref=kv.at[0], dst_ref=kv.at[k], send_sem=kv_send.at[k], recv_sem=kv_recv.at[k],
+            device_id=device(here + 2 * k), device_id_type=MESH,
+        )
+
+    def ret_copy(k):
+        return pltpu.make_async_remote_copy(
+            src_ref=ret_out.at[k], dst_ref=ret_in.at[k], send_sem=ret_send.at[k], recv_sem=ret_recv.at[k],
+            device_id=device(here - 2 * k), device_id_type=MESH,
+        )
+
+    def sib_copy(src, dst, n):
+        return pltpu.make_async_remote_copy(
+            src_ref=src, dst_ref=dst, send_sem=sib_send.at[n], recv_sem=sib_recv.at[n],
+            device_id=sibling, device_id_type=MESH,
+        )
+
+    for k in range(1, REACH + 1):
+        pl.when(ahead(k))(kv_copy(k).start)
+
+    for copy in loads[2:]:
+        copy.wait()
+    to_sib = [sib_copy(qs.at[0], qs.at[1], 0), sib_copy(gs.at[0], gs.at[1], 1)]
+    for copy in to_sib:
+        copy.start()
 
     lane = lax.broadcasted_iota(jnp.int32, (8, TOK), 1)
     first = here * TOK
@@ -76,36 +122,6 @@
         ]
     start[0] = low[0]
     start[1] = low[1]
-
-    pl.semaphore_wait(barrier, 2 * REACH + 1)
-    for copy in loads[:2]:
-        copy.wait()
-
-    def kv_copy(k):
-        return pltpu.make_async_remote_copy(
-            src_ref=kv.at[0], dst_ref=kv.at[k], send_sem=kv_send.at[k], recv_sem=kv_recv.at[k],
-            device_id=device(here + 2 * k), device_id_type=MESH,
-        )
-
-    def ret_copy(k):
-        return pltpu.make_async_remote_copy(
-            src_ref=ret_out.at[k], dst_ref=ret_in.at[k], send_sem=ret_send.at[k], recv_sem=ret_recv.at[k],
-            device_id=device(here - 2 * k), device_id_type=MESH,
-        )
-
-    def sib_copy(src, dst, n):
-        return pltpu.make_async_remote_copy(
-            src_ref=src, dst_ref=dst, send_sem=sib_send.at[n], recv_sem=sib_recv.at[n],
-            device_id=sibling, device_id_type=MESH,
-        )
-
-    for k in range(1, REACH + 1):
-        kv_copy(k).start()
-    for copy in loads[2:]:
-        copy.wait()
-    to_sib = [sib_copy(qs.at[0], qs.at[1], 0), sib_copy(gs.at[0], gs.at[1], 1)]
-    for copy in to_sib:
-        copy.start()
 
     row = lax.broadcasted_iota(jnp.int32, (HEADS, DIM), 0)
     delta = jnp.zeros((HEADS, TOK), F32)
@@ -141,16 +157,28 @@
         acc[:TOK, :] += nn(ds[a, k], qs[a])
         acc[TOK:, :] += nn(probs[...], gs[a])
 
-    def block(k, _):
-        @pl.when(k > 0)
+    y = lax.rem(here // 2, REACH)
+    orders = ((4, 3, 1, 2), (1, 4, 3, 2), (1, 4, 2, 3), (1, 3, 2, 4))
+
+    def block(step, _):
+        k = jnp.int32(0)
+        for place, order in enumerate(orders):
+            for n, back in enumerate(order):
+                k = jnp.where((y == place) & (step == n + 1), back, k)
+
+        @pl.when((k > 0) & behind(k))
         def _():
             kv_copy(k).wait_recv()
+
+        @pl.when((k > 0) & ~behind(k))
+        def _():
+            kv[k] = jnp.zeros_like(kv[k])
 
         kt[k] = kv[k, :TOK, :].T
         acc[...] = jnp.zeros_like(acc)
         pair(k, 0)
 
-        @pl.when(k == core)
+        @pl.when(step == core)
         def _():
             for copy in to_sib:
                 copy.wait_recv()
@@ -165,7 +193,7 @@
         def _():
             own[...] = acc[...]
 
-        @pl.when(k > 0)
+        @pl.when((k > 0) & behind(k))
         def _():
             ret_out[k] = acc[...].astype(BF16)
             ret_copy(k).start()
@@ -188,29 +216,54 @@
         part = sum(nn(kt[m], ds[0, m, :, cols]) for m in range(REACH + 1))
         both = part * scale + dq_in[h].astype(F32)
         dq_fin[:, h * DIM : (h + 1) * DIM] = both.T.astype(BF16)
-    store = pltpu.make_async_copy(dq_fin, dq_hbm, store_sem)
+    store = pltpu.make_async_copy(dq_fin, dq_hbm, store_sem.at[0])
     store.start()
 
-    grads = own[...]
-    for k in range(1, REACH + 1):
-        ret_copy(k).wait_recv()
-        grads = grads + ret_in[k].astype(F32)
-    dk_out[...] = grads[:TOK].astype(BF16)
-    dv_out[...] = grads[TOK:].astype(BF16)
+    for k in range(1, REACH + 1):
+
+        @pl.when(ahead(k))
+        def _():
+            ret_copy(k).wait_recv()
+            own[...] += ret_in[k].astype(F32)
+
+    dkv_fin[...] = own[...].astype(BF16)
+    stores = [store]
+    for n, ref in enumerate((dk_hbm, dv_hbm)):
+        stores.append(pltpu.make_async_copy(dkv_fin.at[pl.ds(n * TOK, TOK)], ref, store_sem.at[n + 1]))
+        stores[-1].start()
 
     dq_copy.wait_send()
     for k in range(1, REACH + 1):
-        kv_copy(k).wait_send()
-        ret_copy(k).wait_send()
-    store.wait()
+        pl.when(ahead(k))(kv_copy(k).wait_send)
+        pl.when(behind(k))(ret_copy(k).wait_send)
+    for copy in stores:
+        copy.wait()
+
+
+def finish(dq_in, dk_in, dv_in, dq_out, dk_out, dv_out, dq, dk, dv, in_sem, out_sem):
+    parts = 4
+    rows = TOK // parts
+    moves = [
+        (dq_in.at[pl.ds(n * rows, rows)], dq.at[pl.ds(n * rows, rows)], dq_out.at[pl.ds(n * rows, rows)])
+        for n in range(parts)
+    ]
+    moves += [(dk_in, dk, dk_out), (dv_in, dv, dv_out)]
+    reads = [pltpu.make_async_copy(a, b, in_sem.at[n]) for n, (a, b, _) in enumerate(moves)]
+    writes = [pltpu.make_async_copy(b, c, out_sem.at[n]) for n, (_, b, c) in enumerate(moves)]
+    for read in reads:
+        read.start()
+    for read, write in zip(reads, writes):
+        read.wait()
+        write.start()
+    for write in writes:
+        write.wait()
 
 
 def local(outer, inner, queries, keys, values, outputs, out_grads, log_sums, doc_lengths):
     wide = HEADS * TOK
     anywhere = pl.BlockSpec(memory_space=pl.ANY)
-    vmem = pl.BlockSpec(memory_space=pltpu.VMEM)
     dma = pltpu.SemaphoreType.DMA
-    return pl.pallas_call(
+    grads = pl.pallas_call(
         functools.partial(kernel, outer, inner),
         out_shape=[
             jax.ShapeDtypeStruct((TOK, HEADS * DIM), BF16),
@@ -218,7 +271,7 @@
             jax.ShapeDtypeStruct((TOK, DIM), BF16),
         ],
         in_specs=[anywhere] * 6 + [pl.BlockSpec(memory_space=pltpu.SMEM)],
-        out_specs=[anywhere, vmem, vmem],
+        out_specs=[anywhere] * 3,
         scratch_shapes=[
             pltpu.VMEM((2, wide, DIM), BF16),
             pltpu.VMEM((2, wide, DIM), BF16),
@@ -237,6 +290,7 @@
             pltpu.VMEM((HEADS, DIM, TOK), BF16),
             pltpu.VMEM((HEADS, DIM, TOK), BF16),
             pltpu.VMEM((TOK, HEADS * DIM), BF16),
+            pltpu.VMEM((2 * TOK, DIM), BF16),
             dma((27,)),
             dma((REACH + 1,)),
             dma((REACH + 1,)),
@@ -244,13 +298,23 @@
             dma((REACH + 1,)),
             dma((4,)),
             dma((4,)),
-            dma,
+            dma((3,)),
         ],
         compiler_params=pltpu.CompilerParams(
-            collective_id=0, has_side_effects=True, vmem_limit_bytes=48 << 20
+            collective_id=0, has_side_effects=True, vmem_limit_bytes=60 << 20
         ),
         name="attention_backward",
     )(queries, keys, values, outputs, out_grads, log_sums, doc_lengths)
+    shapes = [(TOK, HEADS * DIM), (TOK, DIM), (TOK, DIM)]
+    return pl.pallas_call(
+        finish,
+        out_shape=[jax.ShapeDtypeStruct(shape, BF16) for shape in shapes],
+        in_specs=[anywhere] * 3,
+        out_specs=[anywhere] * 3,
+        scratch_shapes=[pltpu.VMEM(shape, BF16) for shape in shapes] + [dma((6,)), dma((6,))],
+        compiler_params=pltpu.CompilerParams(vmem_limit_bytes=60 << 20),
+        name="finish",
+    )(*grads)
 
 
 def solution(mesh):

time: 43.5 us -> 33.9 us (0.78)
  the two profiles are of different devices: /device:TPU:8 before, /device:TPU:126 now
where the time goes in v2:
time: 33.9 us; the launch traced here: 33.7 us
  Pallas kernels  33.1 us (98%)
  between operations  0.64 us (2%)
    pallas_call x1, Pallas kernels, local(): pl.pallas_call(functools.partial(kernel, outer, inner), out_shape=[jax.Sh...  31.2 us
    pallas_call x1, Pallas kernels, local(): pl.pallas_call(finish, out_shape=[jax.ShapeDtypeStruct(shape, BF16) for s...  1.89 us

profile of v2, /device:TPU:126, one launch (start us, length us, event | category | flops | bytes accessed | tf_op | source)
XLA Modules:
  0.0 33.7 jit_solution(13934905421240845209)
XLA Ops:
  0.6 31.2 %attention_backward.1 = (bf16[256,1024]{1,0:T(8,128)(2,1)}, bf16[256,128]{1,0:T(8,128)(2,1)}, bf16[256,128]{1,0:T(8,128)(2,1)}) custom-call(bf16[256,1024]{1,0:T(8,128)(2,1)} %q_hbm.1, bf16[256,128]{1,0:T(8,128)(2,1)} %k_hbm.1, bf16[256,128]{1,0:T(8,128)(2,1)} %v_hbm.1, bf16[256,1024]{1,0:T(8,128)(2,1)} %o_hbm.1, bf16[256,1024]{1,0:T(8,128)(2,1)} %g_hbm.1, ...), custom_call_target="tpu_custom_call" | custom-call | tf_op jit(solution)/shard_map/attention_backward/pallas_call | solution.py:266
  31.8 1.9 %finish.1 = (bf16[256,1024]{1,0:T(8,128)(2,1)}, bf16[256,128]{1,0:T(8,128)(2,1)}, bf16[256,128]{1,0:T(8,128)(2,1)}) custom-call(bf16[256,1024]{1,0:T(8,128)(2,1)} %get-tuple-element.6.dq_in, bf16[256,128]{1,0:T(8,128)(2,1)} %get-tuple-element.7.dk_in, bf16[256,128]{1,0:T(8,128)(2,1)} %get-tuple-element.8.dv_in), custom_call_target="tpu_custom_call" | custom-call | tf_op jit(solution)/shard_map/finish/pallas_call | solution.py:309

commit v3 on v2

v3 whole, which is shorter than its diff:
```python
import functools
import math

import jax
import jax.numpy as jnp
from jax import lax
from jax.experimental import pallas as pl
from jax.experimental.pallas import tpu as pltpu
from jax.sharding import PartitionSpec as P

MESH = pl.DeviceIdType.MESH
F32 = jnp.float32
BF16 = jnp.bfloat16
HEADS = 8
DIM = 128
TOK = 256
GROUP = 2
REACH = 4


def nn(a, b):
    return lax.dot_general(a, b, (((1,), (0,)), ((), ())), preferred_element_type=F32)


def nt(a, b):
    return lax.dot_general(a, b, (((1,), (1,)), ((), ())), preferred_element_type=F32)


def kernel(
    outer, inner, q_hbm, k_hbm, v_hbm, o_hbm, g_hbm, lse_hbm, docs_hbm, dq_fin, own, ret_in,
    docs, qs, gs, qt, gt, os, rows, cols, kv, bias, start, probs, ds, acc, ret_out, dq_out, dq_in,
    load_sem, kv_send, kv_recv, ret_send, ret_recv, sib_send, sib_recv,
):
    dp = lax.axis_index("dp")
    here = lax.axis_index("outer") * inner + lax.axis_index("inner")
    core = lax.rem(here, 2)
    y = lax.rem(here // 2, REACH)
    total = outer * inner
    scale = 1.0 / DIM**0.5
    log2e = math.log2(math.e)

    def device(index):
        index = lax.rem(index + total, total)
        return (dp, index // inner, lax.rem(index, inner))

    sibling = device(here + 1 - 2 * core)

    def ahead(k):
        return here + 2 * k < total

    def behind(k):
        return here - 2 * k >= 0

    barrier = pltpu.get_barrier_semaphore()
    pl.semaphore_signal(barrier, inc=1, device_id=sibling, device_id_type=MESH)
    for k in range(1, REACH + 1):
        for reaches, way in ((ahead, 1), (behind, -1)):

            @pl.when(reaches(k))
            def _():
                pl.semaphore_signal(
                    barrier, inc=1, device_id=device(here + way * 2 * k), device_id_type=MESH
                )

    loads = []

    def load(src, dst, n):
        copy = pltpu.make_async_copy(src, dst, load_sem.at[n])
        copy.start()
        loads.append(copy)

    load(k_hbm, kv.at[0, pl.ds(0, TOK)], 0)
    load(v_hbm, kv.at[0, pl.ds(TOK, TOK)], 1)
    for h in range(HEADS):
        load(q_hbm.at[:, pl.ds(h * DIM, DIM)], qs.at[0, pl.ds(h * TOK, TOK)], 2 + h)
        load(g_hbm.at[:, pl.ds(h * DIM, DIM)], gs.at[0, pl.ds(h * TOK, TOK)], 10 + h)
        load(o_hbm.at[:, pl.ds(h * DIM, DIM)], os.at[pl.ds(h * TOK, TOK)], 18 + h)
    load(lse_hbm, rows.at[0, pl.ds(0, HEADS)], 26)
    load(docs_hbm, docs, 27)

    greeted = jnp.int32(1)
    for k in range(1, REACH + 1):
        for reaches in (ahead, behind):
            greeted = greeted + jnp.where(reaches(k), 1, 0)
    pl.semaphore_wait(barrier, greeted)
    for copy in loads[:2]:
        copy.wait()

    def kv_copy(k):
        return pltpu.make_async_remote_copy(
            src_ref=kv.at[0], dst_ref=kv.at[k], send_sem=kv_send.at[k], recv_sem=kv_recv.at[k],
            device_id=device(here + 2 * k), device_id_type=MESH,
        )

    def ret_copy(k):
        return pltpu.make_async_remote_copy(
            src_ref=ret_out.at[k], dst_ref=ret_in.at[k], send_sem=ret_send.at[k], recv_sem=ret_recv.at[k],
            device_id=device(here - 2 * k), device_id_type=MESH,
        )

    def sib_copy(src, dst, n):
        return pltpu.make_async_remote_copy(
            src_ref=src, dst_ref=dst, send_sem=sib_send.at[n], recv_sem=sib_recv.at[n],
            device_id=sibling, device_id_type=MESH,
        )

    def send(slot):
        def start(k):
            kv_copy(k).start()

        pl.when((slot <= y) & ahead(REACH - y + slot))(lambda: start(REACH - y + slot))
        pl.when(slot + y <= REACH - 2)(lambda: start(slot + 1))

    for z_ in range(4):
        send(z_)
    for copy in loads[2:]:
        copy.wait()
    to_sib = [sib_copy(qs.at[0], qs.at[1], 0), sib_copy(gs.at[0], gs.at[1], 1)]
    for copy in to_sib:
        copy.start()

    line = lax.broadcasted_iota(jnp.int32, (TOK, DIM), 0)
    first = here * TOK
    other = (here + 1 - 2 * core) * TOK
    end = jnp.int32(0)
    low = [jnp.zeros((TOK, DIM), jnp.int32) for _ in range(2)]
    for d in range(docs.shape[0]):
        end = end + docs[d]
        low = [jnp.where(line + base >= end, end, x) for base, x in zip((first, other), low)]
    start[0] = low[0]
    start[1] = low[1]

    row = lax.broadcasted_iota(jnp.int32, (HEADS, DIM), 0)
    delta = jnp.zeros((HEADS, TOK), F32)
    for h in range(HEADS):
        part = pl.ds(h * TOK, TOK)
        prod = gs[0, part, :].astype(F32) * os[part, :].astype(F32)
        hi = prod.astype(BF16)
        lo = (prod - hi.astype(F32)).astype(BF16)
        pick = jnp.where(row == h, 1.0, 0.0).astype(BF16)
        delta = delta + (nt(pick, hi) + nt(pick, lo))
    rows[0, HEADS:, :] = delta
    rows[0, :HEADS, :] = rows[0, :HEADS, :] * log2e
    to_sib.append(sib_copy(rows.at[0], rows.at[1], 2))
    to_sib[2].start()

    def prepare(a):
        left = rows[a]
        terms = []
        for _ in range(3):
            terms.append(left.astype(BF16))
            left = left - terms[-1].astype(F32)
        columns = jnp.concatenate(terms, axis=0).T
        place = lax.broadcasted_iota(jnp.int32, (6 * HEADS, DIM), 0)
        for n in range(2 * HEADS):
            pick = jnp.where(lax.rem(place, 2 * HEADS) == n, 1.0, 0.0).astype(BF16)
            cols[a, n] = nn(columns, pick)
        for h in range(HEADS):
            part = pl.ds(h * TOK, TOK)
            qt[a, :, part] = qs[a, part, :].T
            gt[a, :, part] = gs[a, part, :].T

    def twice(x):
        return jnp.concatenate([x, x], axis=1)

    def pair(k, a):
        query_base = lax.select(a == 0, first, other)
        key_base = (here - 2 * k) * TOK
        p = query_base + lax.broadcasted_iota(jnp.int32, (TOK, TOK), 0)
        t = key_base + lax.broadcasted_iota(jnp.int32, (TOK, TOK), 1)
        ok = (t >= twice(start[a])) & (t <= p)
        bias[...] = jnp.where(ok, 0.0, -jnp.inf)
        keys = kv[k, :TOK, :]
        values = kv[k, TOK:, :]
        for n in range(HEADS // GROUP):
            part = pl.ds(n * GROUP * TOK, GROUP * TOK)
            scores = nt(qs[a, part, :], keys)
            dprob = nt(gs[a, part, :], values)
            for m in range(GROUP):
                h = n * GROUP + m
                mine = slice(m * TOK, (m + 1) * TOK)
                out = pl.ds(h * TOK, TOK)
                prob = jnp.exp2(scores[mine] * (scale * log2e) - twice(cols[a, h]) + bias[...])
                dscore = prob * (dprob[mine] - twice(cols[a, HEADS + h]))
                probs[out, :] = prob.astype(BF16)
                ds[a, k, out, :] = dscore.astype(BF16)
        acc[:DIM, :] += nn(qt[a], ds[a, k])
        acc[DIM:, :] += nn(gt[a], probs[...])

    orders = ((4, 3, 1, 2), (1, 4, 3, 2), (1, 4, 2, 3), (1, 3, 2, 4))

    prepare(0)

    def item(n, _):
        step, a = n // 2, lax.rem(n, 2)
        k = jnp.int32(0)
        for place, order in enumerate(orders):
            for m, back in enumerate(order):
                k = jnp.where((y == place) & (step == m + 1), back, k)

        @pl.when(n == 1)
        def _():
            for copy in to_sib:
                copy.wait_recv()
            prepare(1)


        @pl.when((a == 0) & (k > 0) & behind(k))
        def _():
            kv_copy(k).wait_recv()


        @pl.when((a == 0) & (k > 0) & ~behind(k))
        def _():
            kv[k] = jnp.zeros_like(kv[k])

        @pl.when(a == 0)
        def _():
            acc[...] = jnp.zeros_like(acc)

        @pl.when((a == 0) | ((k >= core) & (k < core + REACH)))
        def _():
            pair(k, a)

        @pl.when((a == 1) & (k == 0))
        def _():
            own[:DIM, :] = acc[:DIM, :] * scale
            own[DIM:, :] = acc[DIM:, :]

        @pl.when((a == 1) & (k > 0) & behind(k))
        def _():
            ret_out[k, :DIM, :] = (acc[:DIM, :] * scale).astype(BF16)
            ret_out[k, DIM:, :] = acc[DIM:, :].astype(BF16)
            ret_copy(k).start()

        return 0

    lax.fori_loop(0, 2 * (REACH + 1), item, 0)

    part = sum(nn(ds[1, core + m], kv[core + m, :TOK, :]) for m in range(REACH))
    dq_out[...] = (part * scale).astype(BF16)
    dq_copy = sib_copy(dq_out, dq_in, 3)
    dq_copy.start()
    for copy in to_sib:
        copy.wait_send()
    part = sum(nn(ds[0, m], kv[m, :TOK, :]) for m in range(REACH + 1)) * scale
    dq_copy.wait_recv()
    both = part + dq_in[...].astype(F32)
    for h in range(HEADS):
        dq_fin[:, h * DIM : (h + 1) * DIM] = both[h * TOK : (h + 1) * TOK].astype(BF16)
    dq_copy.wait_send()
    for k in range(1, REACH + 1):
        pl.when(ahead(k))(kv_copy(k).wait_send)
        pl.when(behind(k))(ret_copy(k).wait_send)
    for k in range(1, REACH + 1):
        pl.when(ahead(k))(ret_copy(k).wait_recv)


def finish(outer, inner, dq, own, ret, dq_out, dk_out, dv_out, dk, dv, sem):
    here = lax.axis_index("outer") * inner + lax.axis_index("inner")
    writes = [
        pltpu.make_async_copy(a, b, sem.at[n])
        for n, (a, b) in enumerate(((dq, dq_out), (dk, dk_out), (dv, dv_out)))
    ]
    writes[0].start()
    total = own[...]
    for k in range(1, REACH + 1):
        total = total + jnp.where(here + 2 * k < outer * inner, ret[k].astype(F32), 0.0)
    dk[...] = total[:DIM, :].T.astype(BF16)
    writes[1].start()
    dv[...] = total[DIM:, :].T.astype(BF16)
    writes[2].start()
    for write in writes:
        write.wait()


def local(outer, inner, queries, keys, values, outputs, out_grads, log_sums, doc_lengths):
    wide = HEADS * TOK
    anywhere = pl.BlockSpec(memory_space=pl.ANY)
    dma = pltpu.SemaphoreType.DMA
    grads = pl.pallas_call(
        functools.partial(kernel, outer, inner),
        out_shape=[
            jax.ShapeDtypeStruct((TOK, HEADS * DIM), BF16),
            jax.ShapeDtypeStruct((2 * DIM, TOK), F32),
            jax.ShapeDtypeStruct((REACH + 1, 2 * DIM, TOK), BF16),
        ],
        in_specs=[anywhere] * 7,
        out_specs=[pl.BlockSpec(memory_space=pltpu.VMEM)] * 3,
        scratch_shapes=[
            pltpu.SMEM(doc_lengths.shape, jnp.int32),
            pltpu.VMEM((2, wide, DIM), BF16),
            pltpu.VMEM((2, wide, DIM), BF16),
            pltpu.VMEM((2, DIM, wide), BF16),
            pltpu.VMEM((2, DIM, wide), BF16),
            pltpu.VMEM((wide, DIM), BF16),
            pltpu.VMEM((2, 2 * HEADS, TOK), F32),
            pltpu.VMEM((2, 2 * HEADS, TOK, DIM), F32),
            pltpu.VMEM((REACH + 1, 2 * TOK, DIM), BF16),
            pltpu.VMEM((TOK, TOK), F32),
            pltpu.VMEM((2, TOK, DIM), jnp.int32),
            pltpu.VMEM((wide, TOK), BF16),
            pltpu.VMEM((2, REACH + 1, wide, TOK), BF16),
            pltpu.VMEM((2 * DIM, TOK), F32),
            pltpu.VMEM((REACH + 1, 2 * DIM, TOK), BF16),
            pltpu.VMEM((wide, DIM), BF16),
            pltpu.VMEM((wide, DIM), BF16),
            dma((28,)),
            dma((REACH + 1,)),
            dma((REACH + 1,)),
            dma((REACH + 1,)),
            dma((REACH + 1,)),
            dma((4,)),
            dma((4,)),
        ],
        compiler_params=pltpu.CompilerParams(
            collective_id=0, has_side_effects=True, vmem_limit_bytes=40 << 20
        ),
        name="attention_backward",
    )(*(pltpu.with_memory_space_constraint(x, pltpu.HBM) for x in (queries, keys, values, outputs, out_grads, log_sums, doc_lengths)))
    shapes = [(TOK, HEADS * DIM), (TOK, DIM), (TOK, DIM)]
    return pl.pallas_call(
        functools.partial(finish, outer, inner),
        out_shape=[jax.ShapeDtypeStruct(shape, BF16) for shape in shapes],
        in_specs=[pl.BlockSpec(memory_space=pltpu.VMEM)] * 3,
        out_specs=[anywhere] * 3,
        scratch_shapes=[pltpu.VMEM((TOK, DIM), BF16), pltpu.VMEM((TOK, DIM), BF16), dma((3,))],
        compiler_params=pltpu.CompilerParams(vmem_limit_bytes=16 << 20),
        name="finish",
    )(*grads)


def solution(mesh):
    rows = P(("dp", "outer", "inner"), None)
    return jax.shard_map(
        functools.partial(local, mesh.shape["outer"], mesh.shape["inner"]),
        mesh=mesh,
        in_specs=(rows,) * 5 + (P(None, ("dp", "outer", "inner")), P("dp")),
        out_specs=(rows,) * 3,
        check_vma=False,
    )
```

time: 33.9 us -> 30.3 us (0.89)
  Pallas kernels: 33.1 us -> 29.5 us
    pallas_call x1, Pallas kernels: 31.2 us -> 28.6 us  [local(): pl.pallas_call(functools.partial(kernel, outer, inner), out_shape=[jax.Sh...]
    pallas_call x1, Pallas kernels: 1.89 us -> 0.87 us  [local(): pl.pallas_call(functools.partial(finish, outer, inner), out_shape=[jax.Sh...]
where the time goes in v3:
time: 30.3 us; the launch traced here: 30.1 us
  Pallas kernels  29.5 us (97%)
  between operations  0.64 us (2%)
    pallas_call x1, Pallas kernels, local(): pl.pallas_call(functools.partial(kernel, outer, inner), out_shape=[jax.Sh...  28.6 us
    pallas_call x1, Pallas kernels, local(): pl.pallas_call(functools.partial(finish, outer, inner), out_shape=[jax.Sh...  0.87 us

profile of v3, /device:TPU:126, one launch (start us, length us, event | category | flops | bytes accessed | tf_op | source)
XLA Modules:
  0.0 30.1 jit_solution(6399968939606128292)
XLA Ops:
  0.6 28.6 %attention_backward.1 = (bf16[256,1024]{1,0:T(8,128)(2,1)S(1)}, f32[256,256]{1,0:T(8,128)S(1)}, bf16[5,256,256]{2,1,0:T(8,128)(2,1)S(1)}) custom-call(bf16[256,1024]{1,0:T(8,128)(2,1)} %q_hbm.1, bf16[256,128]{1,0:T(8,128)(2,1)} %k_hbm.1, bf16[256,128]{1,0:T(8,128)(2,1)} %v_hbm.1, bf16[256,1024]{1,0:T(8,128)(2,1)} %o_hbm.1, bf16[256,1024]{1,0:T(8,128)(2,1)} %g_hbm.1, ...), custom_call_target="tpu_custom_call" | custom-call | tf_op jit(solution)/shard_map/attention_backward/pallas_call | solution.py:281
  29.3 0.9 %finish.1 = (bf16[256,1024]{1,0:T(8,128)(2,1)}, bf16[256,128]{1,0:T(8,128)(2,1)}, bf16[256,128]{1,0:T(8,128)(2,1)}) custom-call(bf16[256,1024]{1,0:T(8,128)(2,1)S(1)} %get-tuple-element.6.dq, f32[256,256]{1,0:T(8,128)S(1)} %get-tuple-element.7.own, bf16[5,256,256]{2,1,0:T(8,128)(2,1)S(1)} %get-tuple-element.8.ret), custom_call_target="tpu_custom_call" | custom-call | tf_op jit(solution)/shard_map/finish/pallas_call | solution.py:322

commit v4 on v3

--- a/solution.py
+++ b/solution.py
@@ -28,7 +28,7 @@
 
 def kernel(
     outer, inner, q_hbm, k_hbm, v_hbm, o_hbm, g_hbm, lse_hbm, docs_hbm, dq_fin, own, ret_in,
-    docs, qs, gs, qt, gt, os, rows, cols, kv, bias, start, probs, ds, acc, ret_out, dq_out, dq_in,
+    docs, qs, gs, qt, gt, os, rows, cols, kv, bias, start, probs, ds, ret_out, dq_out, dq_in,
     load_sem, kv_send, kv_recv, ret_send, ret_recv, sib_send, sib_recv,
 ):
     dp = lax.axis_index("dp")
@@ -157,93 +157,85 @@
             cols[a, n] = nn(columns, pick)
         for h in range(HEADS):
             part = pl.ds(h * TOK, TOK)
-            qt[a, :, part] = qs[a, part, :].T
-            gt[a, :, part] = gs[a, part, :].T
+            flat = pl.ds(a * HEADS * TOK + h * TOK, TOK)
+            qt[:, flat] = qs[a, part, :].T
+            gt[:, flat] = gs[a, part, :].T
 
     def twice(x):
         return jnp.concatenate([x, x], axis=1)
 
-    def pair(k, a):
-        query_base = lax.select(a == 0, first, other)
-        key_base = (here - 2 * k) * TOK
-        p = query_base + lax.broadcasted_iota(jnp.int32, (TOK, TOK), 0)
-        t = key_base + lax.broadcasted_iota(jnp.int32, (TOK, TOK), 1)
-        ok = (t >= twice(start[a])) & (t <= p)
-        bias[...] = jnp.where(ok, 0.0, -jnp.inf)
+    def pairs(k):
         keys = kv[k, :TOK, :]
         values = kv[k, TOK:, :]
-        for n in range(HEADS // GROUP):
-            part = pl.ds(n * GROUP * TOK, GROUP * TOK)
+        t = (here - 2 * k) * TOK + lax.broadcasted_iota(jnp.int32, (TOK, TOK), 1)
+        for a, query_base in enumerate((first, other)):
+            p = query_base + lax.broadcasted_iota(jnp.int32, (TOK, TOK), 0)
+            bias[a] = jnp.where((t >= twice(start[a])) & (t <= p), 0.0, -jnp.inf)
+        for n in range(2 * HEADS // GROUP):
+            a, h0 = n * GROUP // HEADS, n * GROUP % HEADS
+            part = pl.ds(h0 * TOK, GROUP * TOK)
             scores = nt(qs[a, part, :], keys)
             dprob = nt(gs[a, part, :], values)
             for m in range(GROUP):
-                h = n * GROUP + m
+                h = h0 + m
                 mine = slice(m * TOK, (m + 1) * TOK)
-                out = pl.ds(h * TOK, TOK)
-                prob = jnp.exp2(scores[mine] * (scale * log2e) - twice(cols[a, h]) + bias[...])
+                out = pl.ds((a * HEADS + h) * TOK, TOK)
+                prob = jnp.exp2(scores[mine] * (scale * log2e) - twice(cols[a, h]) + bias[a])
                 dscore = prob * (dprob[mine] - twice(cols[a, HEADS + h]))
                 probs[out, :] = prob.astype(BF16)
-                ds[a, k, out, :] = dscore.astype(BF16)
-        acc[:DIM, :] += nn(qt[a], ds[a, k])
-        acc[DIM:, :] += nn(gt[a], probs[...])
+                ds[k, out, :] = dscore.astype(BF16)
+        half = HEADS * TOK
+        dk = nn(qt[:, :half], ds[k, :half, :]) + nn(qt[:, half:], ds[k, half:, :])
+        dv = nn(gt[:, :half], probs[:half, :]) + nn(gt[:, half:], probs[half:, :])
+        return dk * scale, dv
 
     orders = ((4, 3, 1, 2), (1, 4, 3, 2), (1, 4, 2, 3), (1, 3, 2, 4))
 
     prepare(0)
 
-    def item(n, _):
-        step, a = n // 2, lax.rem(n, 2)
+    for copy in to_sib:
+        copy.wait_recv()
+    prepare(1)
+
+    def block(step, _):
         k = jnp.int32(0)
         for place, order in enumerate(orders):
             for m, back in enumerate(order):
                 k = jnp.where((y == place) & (step == m + 1), back, k)
 
-        @pl.when(n == 1)
-        def _():
-            for copy in to_sib:
-                copy.wait_recv()
-            prepare(1)
-
-
-        @pl.when((a == 0) & (k > 0) & behind(k))
+        @pl.when((k > 0) & behind(k))
         def _():
             kv_copy(k).wait_recv()
 
-
-        @pl.when((a == 0) & (k > 0) & ~behind(k))
+        @pl.when((k > 0) & ~behind(k))
         def _():
             kv[k] = jnp.zeros_like(kv[k])
 
-        @pl.when(a == 0)
+        dk, dv = pairs(k)
+
+        @pl.when(k == 0)
         def _():
-            acc[...] = jnp.zeros_like(acc)
-
-        @pl.when((a == 0) | ((k >= core) & (k < core + REACH)))
+            own[:DIM, :] = dk
+            own[DIM:, :] = dv
+
+        @pl.when((k > 0) & behind(k))
         def _():
-            pair(k, a)
-
-        @pl.when((a == 1) & (k == 0))
-        def _():
-            own[:DIM, :] = acc[:DIM, :] * scale
-            own[DIM:, :] = acc[DIM:, :]
-
-        @pl.when((a == 1) & (k > 0) & behind(k))
-        def _():
-            ret_out[k, :DIM, :] = (acc[:DIM, :] * scale).astype(BF16)
-            ret_out[k, DIM:, :] = acc[DIM:, :].astype(BF16)
+            ret_out[k, :DIM, :] = dk.astype(BF16)
+            ret_out[k, DIM:, :] = dv.astype(BF16)
             ret_copy(k).start()
 
         return 0
 
-    lax.fori_loop(0, 2 * (REACH + 1), item, 0)
-
-    part = sum(nn(ds[1, core + m], kv[core + m, :TOK, :]) for m in range(REACH))
+    lax.fori_loop(0, REACH + 1, block, 0)
+
+    half = HEADS * TOK
+    part = sum(nn(ds[core + m, half:, :], kv[core + m, :TOK, :]) for m in range(REACH))
     dq_out[...] = (part * scale).astype(BF16)
     dq_copy = sib_copy(dq_out, dq_in, 3)
     dq_copy.start()
     for copy in to_sib:
         copy.wait_send()
-    part = sum(nn(ds[0, m], kv[m, :TOK, :]) for m in range(REACH + 1)) * scale
+    part = sum(nn(ds[m, :half, :], kv[m, :TOK, :]) for m in range(REACH + 1)) * scale
     dq_copy.wait_recv()
     both = part + dq_in[...].astype(F32)
     for h in range(HEADS):
@@ -291,17 +283,16 @@
             pltpu.SMEM(doc_lengths.shape, jnp.int32),
             pltpu.VMEM((2, wide, DIM), BF16),
             pltpu.VMEM((2, wide, DIM), BF16),
-            pltpu.VMEM((2, DIM, wide), BF16),
-            pltpu.VMEM((2, DIM, wide), BF16),
+            pltpu.VMEM((DIM, 2 * wide), BF16),
+            pltpu.VMEM((DIM, 2 * wide), BF16),
             pltpu.VMEM((wide, DIM), BF16),
             pltpu.VMEM((2, 2 * HEADS, TOK), F32),
             pltpu.VMEM((2, 2 * HEADS, TOK, DIM), F32),
             pltpu.VMEM((REACH + 1, 2 * TOK, DIM), BF16),
-            pltpu.VMEM((TOK, TOK), F32),
+            pltpu.VMEM((2, TOK, TOK), F32),
             pltpu.VMEM((2, TOK, DIM), jnp.int32),
-            pltpu.VMEM((wide, TOK), BF16),
-            pltpu.VMEM((2, REACH + 1, wide, TOK), BF16),
-            pltpu.VMEM((2 * DIM, TOK), F32),
+            pltpu.VMEM((2 * wide, TOK), BF16),
+            pltpu.VMEM((REACH + 1, 2 * wide, TOK), BF16),
             pltpu.VMEM((REACH + 1, 2 * DIM, TOK), BF16),
             pltpu.VMEM((wide, DIM), BF16),
             pltpu.VMEM((wide, DIM), BF16),

time: 30.3 us -> 29.9 us (0.987)
  Pallas kernels: 29.5 us -> 29.1 us
    pallas_call x1, Pallas kernels: 28.6 us -> 28.2 us  [local(): pl.pallas_call(functools.partial(kernel, outer, inner), out_shape=[jax.Sh...]
where the time goes in v4:
time: 29.9 us; the launch traced here: 29.7 us
  Pallas kernels  29.1 us (97%)
  between operations  0.64 us (2%)
    pallas_call x1, Pallas kernels, local(): pl.pallas_call(functools.partial(kernel, outer, inner), out_shape=[jax.Sh...  28.2 us
    pallas_call x1, Pallas kernels, local(): pl.pallas_call(functools.partial(finish, outer, inner), out_shape=[jax.Sh...  0.87 us

profile of v4, /device:TPU:126, one launch (start us, length us, event | category | flops | bytes accessed | tf_op | source)
XLA Modules:
  0.0 29.7 jit_solution(12281278042901577727)
XLA Ops:
  0.6 28.2 %attention_backward.1 = (bf16[256,1024]{1,0:T(8,128)(2,1)S(1)}, f32[256,256]{1,0:T(8,128)S(1)}, bf16[5,256,256]{2,1,0:T(8,128)(2,1)S(1)}) custom-call(bf16[256,1024]{1,0:T(8,128)(2,1)} %q_hbm.1, bf16[256,128]{1,0:T(8,128)(2,1)} %k_hbm.1, bf16[256,128]{1,0:T(8,128)(2,1)} %v_hbm.1, bf16[256,1024]{1,0:T(8,128)(2,1)} %o_hbm.1, bf16[256,1024]{1,0:T(8,128)(2,1)} %g_hbm.1, ...), custom_call_target="tpu_custom_call" | custom-call | tf_op jit(solution)/shard_map/attention_backward/pallas_call | solution.py:273
  28.9 0.9 %finish.1 = (bf16[256,1024]{1,0:T(8,128)(2,1)}, bf16[256,128]{1,0:T(8,128)(2,1)}, bf16[256,128]{1,0:T(8,128)(2,1)}) custom-call(bf16[256,1024]{1,0:T(8,128)(2,1)S(1)} %get-tuple-element.6.dq, f32[256,256]{1,0:T(8,128)S(1)} %get-tuple-element.7.own, bf16[5,256,256]{2,1,0:T(8,128)(2,1)S(1)} %get-tuple-element.8.ret), custom_call_target="tpu_custom_call" | custom-call | tf_op jit(solution)/shard_map/finish/pallas_call | solution.py:313

commit v5 on v4

--- a/solution.py
+++ b/solution.py
@@ -28,7 +28,7 @@
 
 def kernel(
     outer, inner, q_hbm, k_hbm, v_hbm, o_hbm, g_hbm, lse_hbm, docs_hbm, dq_fin, own, ret_in,
-    docs, qs, gs, qt, gt, os, rows, cols, kv, bias, start, probs, ds, ret_out, dq_out, dq_in,
+    docs, qs, gs, qt, gt, os, rows, cols, kv, bias, start, probs, ds, both, ret_out, dq_out, dq_in,
     load_sem, kv_send, kv_recv, ret_send, ret_recv, sib_send, sib_recv,
 ):
     dp = lax.axis_index("dp")
@@ -164,14 +164,14 @@
     def twice(x):
         return jnp.concatenate([x, x], axis=1)
 
-    def pairs(k):
+    def pairs(k, sides):
         keys = kv[k, :TOK, :]
         values = kv[k, TOK:, :]
         t = (here - 2 * k) * TOK + lax.broadcasted_iota(jnp.int32, (TOK, TOK), 1)
-        for a, query_base in enumerate((first, other)):
+        for a, query_base in enumerate((first, other)[:sides]):
             p = query_base + lax.broadcasted_iota(jnp.int32, (TOK, TOK), 0)
             bias[a] = jnp.where((t >= twice(start[a])) & (t <= p), 0.0, -jnp.inf)
-        for n in range(2 * HEADS // GROUP):
+        for n in range(sides * HEADS // GROUP):
             a, h0 = n * GROUP // HEADS, n * GROUP % HEADS
             part = pl.ds(h0 * TOK, GROUP * TOK)
             scores = nt(qs[a, part, :], keys)
@@ -185,9 +185,13 @@
                 probs[out, :] = prob.astype(BF16)
                 ds[k, out, :] = dscore.astype(BF16)
         half = HEADS * TOK
-        dk = nn(qt[:, :half], ds[k, :half, :]) + nn(qt[:, half:], ds[k, half:, :])
-        dv = nn(gt[:, :half], probs[:half, :]) + nn(gt[:, half:], probs[half:, :])
-        return dk * scale, dv
+        dk = nn(qt[:, :half], ds[k, :half, :])
+        dv = nn(gt[:, :half], probs[:half, :])
+        if sides == 2:
+            dk = dk + nn(qt[:, half:], ds[k, half:, :])
+            dv = dv + nn(gt[:, half:], probs[half:, :])
+        both[:DIM, :] = dk * scale
+        both[DIM:, :] = dv
 
     orders = ((4, 3, 1, 2), (1, 4, 3, 2), (1, 4, 2, 3), (1, 3, 2, 4))
 
@@ -211,17 +215,17 @@
         def _():
             kv[k] = jnp.zeros_like(kv[k])
 
-        dk, dv = pairs(k)
+        near = (k >= core) & (k < core + REACH)
+        pl.when(near)(lambda: pairs(k, 2))
+        pl.when(~near)(lambda: pairs(k, 1))
 
         @pl.when(k == 0)
         def _():
-            own[:DIM, :] = dk
-            own[DIM:, :] = dv
+            own[...] = both[...]
 
         @pl.when((k > 0) & behind(k))
         def _():
-            ret_out[k, :DIM, :] = dk.astype(BF16)
-            ret_out[k, DIM:, :] = dv.astype(BF16)
+            ret_out[k] = both[...].astype(BF16)
             ret_copy(k).start()
 
         return 0
@@ -237,9 +241,9 @@
         copy.wait_send()
     part = sum(nn(ds[m, :half, :], kv[m, :TOK, :]) for m in range(REACH + 1)) * scale
     dq_copy.wait_recv()
-    both = part + dq_in[...].astype(F32)
+    query = part + dq_in[...].astype(F32)
     for h in range(HEADS):
-        dq_fin[:, h * DIM : (h + 1) * DIM] = both[h * TOK : (h + 1) * TOK].astype(BF16)
+        dq_fin[:, h * DIM : (h + 1) * DIM] = query[h * TOK : (h + 1) * TOK].astype(BF16)
     dq_copy.wait_send()
     for k in range(1, REACH + 1):
         pl.when(ahead(k))(kv_copy(k).wait_send)
@@ -293,6 +297,7 @@
             pltpu.VMEM((2, TOK, DIM), jnp.int32),
             pltpu.VMEM((2 * wide, TOK), BF16),
             pltpu.VMEM((REACH + 1, 2 * wide, TOK), BF16),
+            pltpu.VMEM((2 * DIM, TOK), F32),
             pltpu.VMEM((REACH + 1, 2 * DIM, TOK), BF16),
             pltpu.VMEM((wide, DIM), BF16),
             pltpu.VMEM((wide, DIM), BF16),

time: 29.9 us -> 29.4 us (0.983)
  Pallas kernels: 29.1 us -> 28.6 us
    pallas_call x1, Pallas kernels: 28.2 us -> 27.8 us  [local(): pl.pallas_call(functools.partial(kernel, outer, inner), out_shape=[jax.Sh...]
where the time goes in v5:
time: 29.4 us; the launch traced here: 29.3 us
  Pallas kernels  28.6 us (97%)
  between operations  0.64 us (2%)
    pallas_call x1, Pallas kernels, local(): pl.pallas_call(functools.partial(kernel, outer, inner), out_shape=[jax.Sh...  27.8 us
    pallas_call x1, Pallas kernels, local(): pl.pallas_call(functools.partial(finish, outer, inner), out_shape=[jax.Sh...  0.87 us

profile of v5, /device:TPU:126, one launch (start us, length us, event | category | flops | bytes accessed | tf_op | source)
XLA Modules:
  0.0 29.3 jit_solution(15301164473558723265)
XLA Ops:
  0.6 27.8 %attention_backward.1 = (bf16[256,1024]{1,0:T(8,128)(2,1)S(1)}, f32[256,256]{1,0:T(8,128)S(1)}, bf16[5,256,256]{2,1,0:T(8,128)(2,1)S(1)}) custom-call(bf16[256,1024]{1,0:T(8,128)(2,1)} %q_hbm.1, bf16[256,128]{1,0:T(8,128)(2,1)} %k_hbm.1, bf16[256,128]{1,0:T(8,128)(2,1)} %v_hbm.1, bf16[256,1024]{1,0:T(8,128)(2,1)} %o_hbm.1, bf16[256,1024]{1,0:T(8,128)(2,1)} %g_hbm.1, ...), custom_call_target="tpu_custom_call" | custom-call | tf_op jit(solution)/shard_map/attention_backward/pallas_call | solution.py:277
  28.4 0.9 %finish.1 = (bf16[256,1024]{1,0:T(8,128)(2,1)}, bf16[256,128]{1,0:T(8,128)(2,1)}, bf16[256,128]{1,0:T(8,128)(2,1)}) custom-call(bf16[256,1024]{1,0:T(8,128)(2,1)S(1)} %get-tuple-element.6.dq, f32[256,256]{1,0:T(8,128)S(1)} %get-tuple-element.7.own, bf16[5,256,256]{2,1,0:T(8,128)(2,1)S(1)} %get-tuple-element.8.ret), custom_call_target="tpu_custom_call" | custom-call | tf_op jit(solution)/shard_map/finish/pallas_call | solution.py:318
